TPU v7x, 32 devices: a whole 2x2x4 slice. The times are simulated.
32 devices in a mesh: grp: 2 (over y), dom: 4 (over z), st: 2 (over x), sub: 2 (over core).
Axes of the slice: x: 2, y: 2, z: 4, core: 2. Of those that a mesh axis runs over, the one named last changes fastest.
Arguments:
- node_feats: bfloat16 [256, 256], P(('grp', 'dom')), parts along dimension 0, may hold values from -6 to 6
- distance: float32 [256, 64], P(('grp', 'dom'), ('st', 'sub')), parts along dimension 0, may hold values from 1.3 to 6.5
- neighbours: int32 [256, 64], P(('grp', 'dom'), ('st', 'sub')), parts along dimension 0, may hold values from 0 to 127, as said below
- counts: int32 [256], P(('grp', 'dom')), parts along dimension 0, may hold values from 16 to 64
- w_source: bfloat16 [256, 256], replicated, may hold values from -0.375 to 0.375
- w_target: bfloat16 [256, 256], replicated, may hold values from -0.375 to 0.375
- w_radial: bfloat16 [128, 256], replicated, may hold values from -0.5 to 0.5
- w_middle: bfloat16 [256, 256], replicated, may hold values from -0.375 to 0.375
- w_output: bfloat16 [256, 169], replicated, may hold values from -0.125 to 0.125
- w_onsite: bfloat16 [256, 169], replicated, may hold values from -0.375 to 0.375
- initial: float32 [256, 13, 128], P(('grp', 'dom')), parts along dimension 0, may hold values from -100 to 100
Outputs:
- alpha_blocks: float32 [4, 128, 128], P('grp'), parts along dimension 0
- beta_blocks: float32 [4, 128, 128], P('grp'), parts along dimension 0
- next_states: float32 [256, 13, 128], P(('grp', 'dom')), parts along dimension 0
There are 2 independent parts, one for each index of `grp`. A program takes and returns all parts, laid end to end along the dimension named above; an argument that names none is the same for every part. Nothing has to cross between parts.
Inputs may be any that keep to these rules, and one draw needn't show every extreme that they name: `neighbours`: every partner lies in the atom's own domain of 32 consecutive atoms (never the atom itself) or in the next domain, the last domain's next being the first.
All inputs are finite; a program needn't handle non-finite values.
Results may differ from a plain program's by a relative error of at most 0.014.
Values may be sent and summed in bfloat16 or wider, within the bound.
No kernel may reach another device: no remote copies, remote signals or barrier semaphores. Data moves between devices by JAX's collectives and lax.ppermute only.
A program may use at most 64 MiB of HBM per device.

v0:
```python
import jax
import jax.numpy as jnp
from jax import lax
from jax.sharding import PartitionSpec as P

ORB = 13
STEPS = 2


RADIUS = 7.0


def shifted(shard, axis, by):
    devices = lax.axis_size(axis)
    return lax.ppermute(shard, axis, [(i, (i + by) % devices) for i in range(devices)])


def radial(distance, basis_count):
    centres = RADIUS * jnp.arange(basis_count, dtype=jnp.float32) / basis_count
    spacing = RADIUS / basis_count
    return jnp.exp(-jnp.square((distance[..., None] - centres) / (2.0 * spacing)))


def envelope(distance, usable):
    return 0.5 * (jnp.cos(jnp.pi * distance / RADIUS) + 1.0) * usable.astype(jnp.float32)


def onsite_blocks(node_feats, w_onsite):
    projected = jnp.dot(node_feats, w_onsite, preferred_element_type=jnp.float32)
    matrix = projected.reshape(-1, ORB, ORB)
    return (0.5 * (matrix + jnp.swapaxes(matrix, 1, 2))).astype(jnp.bfloat16)


def pair_blocks(source_rows, target_rows, distance, usable, w_radial, w_middle, w_output):
    radial_basis = radial(distance, w_radial.shape[0]).astype(jnp.bfloat16)
    mixed = source_rows[:, None, :].astype(jnp.float32) + target_rows.astype(jnp.float32)
    mixed = mixed + jnp.dot(radial_basis, w_radial, preferred_element_type=jnp.float32)
    hidden_one = jax.nn.silu(mixed).astype(jnp.bfloat16)
    second = jax.nn.silu(jnp.dot(hidden_one, w_middle, preferred_element_type=jnp.float32)).astype(
        jnp.bfloat16
    )
    output_blocks = (
        jnp.dot(second, w_output, preferred_element_type=jnp.float32)
        * envelope(distance, usable)[..., None]
    )
    return output_blocks.astype(jnp.bfloat16).reshape(
        distance.shape[0], distance.shape[1], ORB, ORB
    )


def gram_matrix(left, right, rows_total):
    return jnp.einsum("ris,rit->st", left, right, precision=lax.Precision.HIGHEST) / rows_total


def combine(states, matrix):
    return jnp.einsum("ris,st->rit", states, matrix, precision=lax.Precision.HIGHEST)


def upper_factor(matrix):
    order = matrix.shape[0]
    places = jnp.arange(order, dtype=jnp.int32)

    def column_step(column_index, carry):
        work, lower = carry
        column = lax.dynamic_slice_in_dim(work, column_index, 1, 1)[:, 0]
        pivot = jnp.sqrt(lax.dynamic_slice_in_dim(column, column_index, 1, 0)[0])
        scaled = jnp.where(places >= column_index, column / pivot, jnp.zeros_like(column))
        work = work - scaled[:, None] * scaled[None, :]
        lower = lax.dynamic_update_slice_in_dim(lower, scaled[:, None], column_index, 1)
        return (work, lower)

    work, lower = lax.fori_loop(0, order, column_step, (matrix, jnp.zeros_like(matrix)))
    return lower.T


def upper_inverse(factor):
    order = factor.shape[0]
    identity = jnp.eye(order, dtype=factor.dtype)

    def row_step(counter, inverse):
        row_index = order - 1 - counter
        factor_row = lax.dynamic_slice_in_dim(factor, row_index, 1, 0)
        unit_row = lax.dynamic_slice_in_dim(identity, row_index, 1, 0)
        pivot = lax.dynamic_slice_in_dim(factor_row[0], row_index, 1, 0)[0]
        known = jnp.dot(factor_row, inverse, precision=lax.Precision.HIGHEST)
        fresh = (unit_row - known) / pivot
        return lax.dynamic_update_slice_in_dim(inverse, fresh, row_index, 0)

    return lax.fori_loop(0, order, row_step, jnp.zeros_like(factor))


def divide_right(residue, factor):
    return combine(residue, upper_inverse(factor))


def onsite_apply(onsite, states):
    return jnp.einsum("aij,ajs->ais", onsite, states, precision=lax.Precision.HIGHEST)


def lanczos(states, operate, totals, rows_total):
    factor = upper_factor(totals(gram_matrix(states, states, rows_total)))
    current = divide_right(states, factor)
    previous = current
    beta_prev = factor
    alpha_list = []
    beta_list = []
    for iteration in range(STEPS):
        residue = operate(current)
        if iteration > 0:
            residue = residue - combine(previous, beta_prev.T)
        alpha_block = totals(gram_matrix(current, residue, rows_total))
        residue = residue - combine(current, alpha_block)
        beta_block = upper_factor(totals(gram_matrix(residue, residue, rows_total)))
        previous = current
        current = divide_right(residue, beta_block)
        beta_prev = beta_block
        alpha_list.append(alpha_block)
        beta_list.append(beta_block)
    return (jnp.stack(alpha_list), jnp.stack(beta_list), current)


def body(
    node_feats,
    distance,
    neighbours,
    counts,
    w_source,
    w_target,
    w_radial,
    w_middle,
    w_output,
    w_onsite,
    initial,
):
    atoms_here = node_feats.shape[0]
    slots_here = neighbours.shape[1]
    domain = lax.axis_index("dom")
    member = lax.axis_index(("st", "sub"))
    atoms_all = atoms_here * lax.axis_size("dom")
    rows_total = float(atoms_all * ORB)
    ghost_feats = shifted(node_feats, "dom", -1)
    local_index = (neighbours - domain * atoms_here) % atoms_all
    source = jnp.dot(node_feats, w_source, preferred_element_type=jnp.float32).astype(jnp.bfloat16)
    combined_feats = jnp.concatenate([node_feats, ghost_feats], axis=0)
    target = jnp.dot(combined_feats, w_target, preferred_element_type=jnp.float32).astype(
        jnp.bfloat16
    )
    slot_index = member * slots_here + jnp.arange(slots_here, dtype=jnp.int32)
    usable = slot_index[None, :] < counts[:, None]
    blocks = pair_blocks(
        source, target[local_index], distance, usable, w_radial, w_middle, w_output
    ).astype(jnp.float32)

    def edge_terms(whole_rows, ghost_rows):
        combined = jnp.concatenate([whole_rows, ghost_rows], axis=0)
        forward = jnp.einsum(
            "akij,akjs->ais", blocks, combined[local_index], precision=lax.Precision.HIGHEST
        )
        backward = jnp.einsum("akij,ais->akjs", blocks, whole_rows, precision=lax.Precision.HIGHEST)
        spread = jax.ops.segment_sum(
            backward.reshape(-1, ORB, whole_rows.shape[-1]),
            local_index.reshape(-1),
            num_segments=2 * atoms_here,
        )
        arrived = shifted(spread[atoms_here:], "dom", 1)
        return forward + spread[:atoms_here] + arrived

    onsite = onsite_blocks(node_feats, w_onsite).astype(jnp.float32)

    def operate(current):
        ghost_rows = shifted(current, "dom", -1)
        summed = lax.psum(edge_terms(current, ghost_rows), ("st", "sub"))
        return summed + onsite_apply(onsite, current)

    def totals(value):
        return lax.psum(value, "dom")

    alpha_blocks, beta_blocks, final_rows = lanczos(initial, operate, totals, rows_total)
    return (alpha_blocks, beta_blocks, final_rows)


def solution(mesh):
    placed = (
        P(("grp", "dom"), None),
        P(("grp", "dom"), ("st", "sub")),
        P(("grp", "dom"), ("st", "sub")),
        P(("grp", "dom")),
        P(),
        P(),
        P(),
        P(),
        P(),
        P(),
        P(("grp", "dom"), None, None),
    )
    return jax.shard_map(
        body,
        mesh=mesh,
        in_specs=placed,
        out_specs=(P("grp", None, None), P("grp", None, None), P(("grp", "dom"), None, None)),
        check_vma=False,
    )
```

profile of v0, /device:TPU:0, one launch (start us, length us, event | category | flops | bytes accessed | tf_op | source)
XLA Modules:
  0.0 1602.8 jit_solution(4802708080698115037)
XLA Ops:
  9.5 5.1 collective-permute-start
  20.8 2.0 gather_fusion
  24.4 2.6 copy.193
  26.9 4.0 copy.161
  30.9 16.7 %all-reduce.8.cloned.1.call-done = f32[128,128]{1,0:T(8,128)} async-done(((f32[128,128]{1,0:T(8,128)}), f32[128,128]{1,0:T(8,128)}) %all-reduce.8.cloned.1.call-update) | async-done | bytes 65552 | tf_op jit(solution)/shard_map/psum | solution.py:176
  48.6 186.7 %while.108 = (s32[]{:T(128)}, f32[128,128]{0,1:T(8,128)S(1)}, f32[128,128]{0,1:T(8,128)S(1)}, s32[]{:T(128)}, s32[]{:T(128)}, /*index=5*/s32[]{:T(128)}) while((s32[]{:T(128)}, f32[128,128]{0,1:T(8,128)S(1)}, f32[128,128]{0,1:T(8,128)S(1)}, s32[]{:T(128)}, s32[]{:T(128)}, /*index=5*/s32[]{:T(128)}) %tuple.264), condition=%wide.region_2.3_spmd.clone, body=%wide.region_1.2_spmd.clone.sunk | while | flops 33411 | bytes 136829 | solution.py:72
  235.4 185.1 %while.105 = (s32[]{:T(128)}, f32[128,128]{1,0:T(8,128)S(1)}, f32[128,128]{1,0:T(8,128)S(1)}, f32[128,128]{1,0:T(8,128)S(1)}, s32[]{:T(128)}, /*index=5*/s32[]{:T(128)}, s32[]{:T(128)}, s32[]{:T(128)}) while((s32[]{:T(128)}, f32[128,128]{1,0:T(8,128)S(1)}, f32[128,128]{1,0:T(8,128)S(1)}, f32[128,128]{1,0:T(8,128)S(1)}, s32[]{:T(128)}, ...), condition=%wide.region_4.5_spmd, body=%wide.region_3.4_spmd.sunk | while | flops 196871 | bytes 69295 | solution.py:89
  420.8 2.2 collective-permute-start.1
  422.9 3.1 fusion.29
  426.0 4.0 copy.166
  430.0 40.2 %scatter_fusion = f32[64,13,128]{2,1,0:T(8,128)S(1)} fusion(f32[64,13,128]{2,1,0:T(8,128)S(1)} %broadcast.257.clone, s32[512]{0:T(512)S(1)} %reshape.229, f32[512,13,128]{2,1,0:T(8,128)} %copy.166), kind=kCustom, calls=%fused_computation.3 | custom fusion | flops 851968 | bytes 10225664 | tf_op jit(solution)/shard_map/scatter-add | solution.py:160
  472.5 3.1 gather_fusion.1
  475.6 5.7 convolution_bitcast_fusion.1
  481.3 1.8 fusion.33
  483.6 32.2 %all-reduce.10.cloned.1.call-done = f32[32,13,128]{2,0,1:T(8,128)} async-done(((f32[32,13,128]{2,0,1:T(8,128)}), f32[32,13,128]{2,0,1:T(8,128)}) %all-reduce.10.cloned.1.call-update) | async-done | bytes 213008 | tf_op jit(solution)/shard_map/psum | solution.py:172
  515.8 2.3 fusion.22
  518.1 35.3 %all-reduce.12.cloned.1.call-done = f32[128,128]{1,0:T(8,128)} async-done(((f32[128,128]{1,0:T(8,128)}), f32[128,128]{1,0:T(8,128)}) %all-reduce.12.cloned.1.call-update) | async-done | bytes 65552 | tf_op jit(solution)/shard_map/psum | solution.py:176
  556.1 33.9 %all-reduce.14.cloned.1.call-done = f32[128,128]{1,0:T(8,128)} async-done(((f32[128,128]{1,0:T(8,128)}), f32[128,128]{1,0:T(8,128)}) %all-reduce.14.cloned.1.call-update) | async-done | bytes 65552 | tf_op jit(solution)/shard_map/psum | solution.py:176
  590.9 186.7 %while.109 = (s32[]{:T(128)}, f32[128,128]{0,1:T(8,128)S(1)}, f32[128,128]{0,1:T(8,128)S(1)}, s32[]{:T(128)}, s32[]{:T(128)}, /*index=5*/s32[]{:T(128)}) while((s32[]{:T(128)}, f32[128,128]{0,1:T(8,128)S(1)}, f32[128,128]{0,1:T(8,128)S(1)}, s32[]{:T(128)}, s32[]{:T(128)}, /*index=5*/s32[]{:T(128)}) %tuple.270), condition=%wide.region_10.11_spmd.clone, body=%wide.region_9.10_spmd.clone.sunk | while | flops 33411 | bytes 136829 | solution.py:72
  777.7 185.1 %while.106 = (s32[]{:T(128)}, f32[128,128]{1,0:T(8,128)S(1)}, f32[128,128]{1,0:T(8,128)S(1)}, f32[128,128]{1,0:T(8,128)S(1)}, s32[]{:T(128)}, /*index=5*/s32[]{:T(128)}, s32[]{:T(128)}, s32[]{:T(128)}) while((s32[]{:T(128)}, f32[128,128]{1,0:T(8,128)S(1)}, f32[128,128]{1,0:T(8,128)S(1)}, f32[128,128]{1,0:T(8,128)S(1)}, s32[]{:T(128)}, ...), condition=%wide.region_12.13_spmd, body=%wide.region_11.12_spmd.sunk | while | flops 196871 | bytes 69295 | solution.py:89
  963.7 3.1 fusion.30
  966.8 2.2 collective-permute-start.3
  968.9 4.0 copy.182
  972.9 40.2 %scatter_fusion.1 = f32[64,13,128]{2,1,0:T(8,128)S(1)} fusion(f32[64,13,128]{2,1,0:T(8,128)S(1)} %broadcast.257, s32[512]{0:T(512)S(1)} %reshape.229, f32[512,13,128]{2,1,0:T(8,128)} %copy.182), kind=kCustom, calls=%fused_computation.4 | custom fusion | flops 851968 | bytes 10225664 | tf_op jit(solution)/shard_map/scatter-add | solution.py:160
  1017.0 3.1 gather_fusion.2
  1020.1 5.8 convolution_bitcast_fusion
  1025.9 1.8 fusion.32
  1028.1 32.2 %all-reduce.16.cloned.1.call-done = f32[32,13,128]{2,0,1:T(8,128)} async-done(((f32[32,13,128]{2,0,1:T(8,128)}), f32[32,13,128]{2,0,1:T(8,128)}) %all-reduce.16.cloned.1.call-update) | async-done | bytes 213008 | tf_op jit(solution)/shard_map/psum | solution.py:172
  1062.7 35.2 %all-reduce.18.cloned.1.call-done = f32[128,128]{1,0:T(8,128)} async-done(((f32[128,128]{1,0:T(8,128)}), f32[128,128]{1,0:T(8,128)}) %all-reduce.18.cloned.1.call-update) | async-done | bytes 65552 | tf_op jit(solution)/shard_map/psum | solution.py:176
  1100.4 1.5 pad_maximum_fusion.2
  1101.9 32.6 %all-reduce.20.cloned.1.call-done = f32[128,128]{1,0:T(8,128)} async-done(((f32[128,128]{1,0:T(8,128)}), f32[128,128]{1,0:T(8,128)}) %all-reduce.20.cloned.1.call-update) | async-done | bytes 65552 | tf_op jit(solution)/shard_map/psum | solution.py:176
  1135.4 186.7 %while.110 = (s32[]{:T(128)}, f32[128,128]{0,1:T(8,128)S(1)}, f32[128,128]{0,1:T(8,128)S(1)}, s32[]{:T(128)}, s32[]{:T(128)}, /*index=5*/s32[]{:T(128)}) while((s32[]{:T(128)}, f32[128,128]{0,1:T(8,128)S(1)}, f32[128,128]{0,1:T(8,128)S(1)}, s32[]{:T(128)}, s32[]{:T(128)}, /*index=5*/s32[]{:T(128)}) %tuple.276), condition=%wide.region_18.19_spmd.clone, body=%wide.region_17.18_spmd.clone.sunk | while | flops 33411 | bytes 136829 | solution.py:72
  1322.2 272.1 %while.107 = (s32[]{:T(128)}, f32[128,128]{1,0:T(8,128)S(1)}, f32[128,128]{1,0:T(8,128)}, f32[128,128]{1,0:T(8,128)S(1)}, s32[]{:T(128)}, /*index=5*/s32[]{:T(128)}, s32[]{:T(128)}, s32[]{:T(128)}) while((s32[]{:T(128)}, f32[128,128]{1,0:T(8,128)S(1)}, f32[128,128]{1,0:T(8,128)}, f32[128,128]{1,0:T(8,128)S(1)}, s32[]{:T(128)}, ...), condition=%wide.region_20.21_spmd, body=%wide.region_19.20_spmd.sunk | while | flops 196871 | bytes 69295 | solution.py:89
  1407.9 1.5 fusion.113
  1410.0 1.5 fusion.113
  1412.1 1.5 fusion.113
  1414.3 1.5 fusion.113
  1416.4 1.5 fusion.113
  1418.5 1.5 fusion.113
  1422.8 1.5 fusion.113
  1526.9 1.5 fusion.113
  1529.1 1.5 fusion.113
  1531.2 1.5 fusion.113
  1533.3 1.5 fusion.113
  1535.5 1.5 fusion.113
  1537.6 1.5 fusion.113
  1539.7 1.5 fusion.113
  1541.9 1.5 fusion.113
  (3154 shorter events, 917.8 us)
Async XLA Ops:
  7.2 0.9 copy-start
  7.2 15.6 copy-start.10
  7.2 15.9 copy-start.8
  7.2 15.9 copy-start.9
  7.2 40.4 %all-reduce.8.cloned.1.call-start = ((), (), s32[]{:S(2)}) async-start(), calls=%async_computation | async-start | bytes 131072 | tf_op jit(solution)/shard_map/psum | solution.py:176
  9.4 506.3 %all-reduce.10.cloned.1.call-start = ((), (), s32[]{:S(2)}) async-start(), calls=%async_computation.1 | async-start | bytes 425984 | tf_op jit(solution)/shard_map/psum | solution.py:172
  9.5 10.2 collective-permute-start
  420.8 50.5 %collective-permute-start.1 = (f32[32,13,128]{2,0,1:T(8,128)S(1)}, f32[32,13,128]{2,0,1:T(8,128)}, u32[]{:S(2)}, u32[]{:S(2)}) collective-permute-start(f32[32,13,128]{2,0,1:T(8,128)S(1)} %convolution_bitcast_fusion.2), channel_id=1, source_target_pairs={{0,12},{4,0},{8,4},{12,8},{1,13},{5,1},{9,5},{13,9},{2,14},{6,2},{... | collective-permute-start | bytes 638984 | tf_op jit(solution)/shard_map/ppermute | solution.py:15
  471.0 10.3 collective-permute-start.2
  475.6 5.7 copy-start.3
  483.1 70.3 %all-reduce.12.cloned.1.call-start = ((), (), s32[]{:S(2)}) async-start(), calls=%async_computation.2 | async-start | bytes 131072 | tf_op jit(solution)/shard_map/psum | solution.py:176
  518.0 71.9 %all-reduce.14.cloned.1.call-start = ((), (), s32[]{:S(2)}) async-start(), calls=%async_computation.3 | async-start | bytes 131072 | tf_op jit(solution)/shard_map/psum | solution.py:176
  556.0 504.3 %all-reduce.16.cloned.1.call-start = ((), (), s32[]{:S(2)}) async-start(), calls=%async_computation.4 | async-start | bytes 425984 | tf_op jit(solution)/shard_map/psum | solution.py:172
  962.7 0.6 copy-start.4
  963.4 9.5 copy-start.7
  966.8 49.0 %collective-permute-start.3 = (f32[32,13,128]{2,0,1:T(8,128)S(1)}, f32[32,13,128]{2,0,1:T(8,128)}, u32[]{:S(2)}, u32[]{:S(2)}) collective-permute-start(f32[32,13,128]{2,0,1:T(8,128)S(1)} %fusion.48), channel_id=1, source_target_pairs={{0,12},{4,0},{8,4},{12,8},{1,13},{5,1},{9,5},{13,9},{2,14},{6,2},{... | collective-permute-start | bytes 638984 | tf_op jit(solution)/shard_map/ppermute | solution.py:15
  1014.7 11.2 collective-permute-start.4
  1020.1 5.8 copy-start.2
  1020.1 7.6 copy-start.5
  1020.1 40.2 %copy-start.1 = (f32[32,13,128]{2,1,0:T(8,128)S(1)}, f32[32,13,128]{2,1,0:T(8,128)}, u32[]{:S(2)}) copy-start(f32[32,13,128]{2,1,0:T(8,128)} %fusion.25) | copy-start | bytes 638980
  1025.8 74.6 %copy-start.6 = (f32[128,128]{1,0:T(8,128)S(1)}, f32[128,128]{1,0:T(8,128)}, u32[]{:S(2)}) copy-start(f32[128,128]{1,0:T(8,128)} %all-reduce.12.cloned.1.call-done) | copy-start | bytes 196612
  1027.7 70.2 %all-reduce.18.cloned.1.call-start = ((), (), s32[]{:S(2)}) async-start(), calls=%async_computation.5 | async-start | bytes 131072 | tf_op jit(solution)/shard_map/psum | solution.py:176
  1062.7 71.8 %all-reduce.20.cloned.1.call-start = ((), (), s32[]{:S(2)}) async-start(), calls=%async_computation.6 | async-start | bytes 131072 | tf_op jit(solution)/shard_map/psum | solution.py:176
Sparse Core Ops, SparseCore 0:
  10.9 36.6 all-reduce.7
  483.2 32.4 all-reduce.9
  518.6 34.6 all-reduce.11
  556.2 33.6 all-reduce.13
  1027.8 32.4 all-reduce.15
  1063.2 34.6 all-reduce.17
  1100.8 33.6 all-reduce.19
where the time goes:
time: 1620 us; the launch traced here: 1600 us
  local copies, waits for them, and re-layouts  510 us (31%)
  matrix products  428 us (26%)
  loops' own time  293 us (18%)
  waiting for transfers between devices  218 us (13%)
  other arithmetic  129 us (8%)
    dot_general x384, matrix products, row_step(): known = jnp.dot(factor_row, inverse, precision=lax.Precision.HIGHEST)  393 us
    another operation x3, loops' own time, upper_factor(): lax.fori_loop(0, order, column_step, (matrix, jnp.zeros_like(matrix)))  282 us
    dynamic_slice x384, local copies, waits for them, and re-layouts, column_step(): pivot = jnp.sqrt(lax.dynamic_slice_in_dim(column, column_index, 1, 0)[0])  226 us
    dynamic_slice x384, local copies, waits for them, and re-layouts, row_step(): pivot = lax.dynamic_slice_in_dim(factor_row[0], row_index, 1, 0)[0]  226 us
    psum x5, waiting for transfers between devices, totals(): return lax.psum(value, 'dom')  154 us
    scatter-add x2, other arithmetic, edge_terms(): jax.ops.segment_sum(backward.reshape(-1, ORB, whole_rows.shape[-1]), loca...  80.4 us
    psum x2, waiting for transfers between devices, operate(): summed = lax.psum(edge_terms(current, ghost_rows), ('st', 'sub'))  64.5 us
  transfers between devices with their start and end apart: 12, of which 7 were waited for; matrix products, arithmetic and copies ran while one was open for 8% of the time, Pallas kernels for 0%

commit v1 on v0

--- a/solution.py
+++ b/solution.py
@@ -1,6 +1,8 @@
 import jax
 import jax.numpy as jnp
 from jax import lax
+from jax.experimental import pallas as pl
+from jax.experimental.pallas import tpu as pltpu
 from jax.sharding import PartitionSpec as P
 
 ORB = 13
@@ -119,7 +121,7 @@
     return (jnp.stack(alpha_list), jnp.stack(beta_list), current)
 
 
-def body(
+def body_spread(
     node_feats,
     distance,
     neighbours,
@@ -179,6 +181,504 @@
     return (alpha_blocks, beta_blocks, final_rows)
 
 
+F32 = jnp.float32
+BF16 = jnp.bfloat16
+LANES = 128
+PAD = 16
+PANEL = 8
+VMEM_LIMIT = 56 * 1024 * 1024
+
+
+def dims(left, right):
+    return (((left,), (right,)), ((), ()))
+
+
+def dot(left, right, contract):
+    return lax.dot_general(left, right, contract, preferred_element_type=F32)
+
+
+def split(value):
+    high = value.astype(BF16)
+    return high, (value - high.astype(F32)).astype(BF16)
+
+
+def dot_split(left, right, contract):
+    lh, ll = left
+    rh, rl = right
+    return dot(lh, rh, contract) + (dot(ll, rh, contract) + dot(lh, rl, contract))
+
+
+NN = dims(1, 0)
+NT = dims(1, 1)
+TN = dims(0, 0)
+
+
+def silu(value):
+    half = 0.5 * value
+    return half + half * jnp.tanh(half)
+
+
+def spread_rows(value, row, count):
+    return jnp.broadcast_to(value[row : row + 1, :], (count, value.shape[1]))
+
+
+def network_kernel(
+    place_ref,
+    lane0,
+    lane1,
+    lane2,
+    lane3,
+    feat0,
+    feat1,
+    feat2,
+    feat3,
+    w_source,
+    w_target,
+    w_radial,
+    w_middle_t,
+    w_output_t,
+    w_onsite_a,
+    w_onsite_b,
+    out_ref,
+    pairs,
+    envelopes,
+    source,
+    target,
+    onsite,
+    mixer,
+):
+    domain = pl.program_id(0)
+    quarter = pl.program_id(1)
+    atoms = feat0.shape[0]
+    half_atoms = atoms // 2
+    tiles = half_atoms // pl.num_programs(1)
+    domains = 4
+    basis = w_radial.shape[0]
+
+    @pl.when((domain == 0) & (quarter == 0))
+    def prepare():
+        place = place_ref[0]
+        lanes = (lane0, lane1, lane2, lane3)
+        feats = (feat0, feat1, feat2, feat3)
+        for step in range(domains):
+            where = place ^ step
+            pairs[where] = lanes[step][...]
+            reach = lanes[step][0]
+            envelopes[where] = 0.5 * (jnp.cos(jnp.pi * reach / RADIUS) + 1.0)
+            rows = feats[step][...]
+            source[where] = dot(rows, w_source[...], NN)
+            target[where] = dot(rows, w_target[...], NN)
+            first = dot(rows, w_onsite_a[...], NN)
+            second = dot(rows, w_onsite_b[...], NN)
+            onsite[pl.ds(where * atoms, atoms), :] = 0.5 * (first + second)
+        turned = onsite[...].astype(BF16).astype(F32)
+        for column in range(onsite.shape[1] // LANES):
+            piece = slice(column * LANES, (column + 1) * LANES)
+            onsite[:, piece] = 0.5 * jnp.transpose(turned[:, piece])
+
+    @pl.when(quarter == 0)
+    def mix():
+        following = lax.rem(domain + 1, domains)
+        mixer[0:basis] = w_radial[...].astype(F32)
+        mixer[basis : basis + atoms] = target[domain]
+        mixer[basis + atoms : basis + 2 * atoms] = target[following]
+        mixer[basis + 2 * atoms : basis + 3 * atoms] = source[domain]
+        mixer[basis + 3 * atoms :] = jnp.zeros((mixer.shape[0] - basis - 3 * atoms, mixer.shape[1]), F32)
+        mixer[...] = jnp.transpose(mixer[...])
+
+    first_tile = quarter * tiles
+    lane = lax.broadcasted_iota(jnp.int32, (1, LANES), 1)
+    upper = lane >= LANES // 2
+    sub128 = lax.broadcasted_iota(jnp.int32, (basis, LANES), 0)
+    centres = RADIUS * sub128.astype(F32) / basis
+    scale = 1.0 / (2.0 * RADIUS / basis)
+    inputs = []
+    envs = []
+    names = []
+    for u in range(tiles):
+        reach = pairs[domain, 0, pl.ds(first_tile + u, 1), :]
+        name = pairs[domain, 1, pl.ds(first_tile + u, 1), :].astype(jnp.int32)
+        envs.append(envelopes[domain, pl.ds(first_tile + u, 1), :])
+        names.append(name)
+        radial_t = jnp.exp(-jnp.square((reach - centres) * scale))
+        local = lax.rem(name - domain * atoms + domains * atoms, domains * atoms)
+        who = first_tile + u + jnp.where(upper, half_atoms, 0)
+        near = sub128[: 2 * atoms] == local
+        mine = sub128[: 2 * atoms] == who
+        inputs.append(
+            jnp.concatenate(
+                [radial_t, jnp.where(near, 1.0, 0.0), jnp.where(mine, 1.0, 0.0)], axis=0
+            ).astype(BF16)
+        )
+    columns = jnp.concatenate(inputs, axis=1)
+    hidden = silu(dot(mixer[...].astype(BF16), columns, NN)).astype(BF16)
+    second = silu(dot(w_middle_t[...], hidden, NN)).astype(BF16)
+    blocks = dot(w_output_t[...], second, NN)
+    row2 = lax.broadcasted_iota(jnp.int32, (LANES, LANES), 0)
+    column2 = lax.broadcasted_iota(jnp.int32, (LANES, LANES), 1)
+    flags = jnp.concatenate(
+        [jnp.where(column2 < LANES // 2, row2, -2), jnp.where(column2 < LANES // 2, -2, row2)], axis=0
+    )
+    for u in range(tiles):
+        piece = (blocks[:, u * LANES : (u + 1) * LANES] * envs[u]).astype(BF16)
+        chosen = jnp.where(flags == names[u], 1.0, 0.0).astype(BF16)
+        placed = dot(piece, chosen, NT)
+        for h in range(2):
+            atom = domain * atoms + h * half_atoms + first_tile + u
+            whole = placed[:, h * LANES : (h + 1) * LANES]
+            for j in range(ORB):
+                part = whole[j * PAD : (j + 1) * PAD]
+                own = onsite_part(onsite, j)
+                part = part + jnp.where(lane == atom, own, 0.0)
+                out_ref[0, h, u * PAD : (u + 1) * PAD, j * LANES : (j + 1) * LANES] = part.astype(BF16)
+
+
+def onsite_part(onsite, j):
+    rows = j * PAD
+    column = rows // LANES
+    start = rows - column * LANES
+    return onsite[start : start + PAD, column * LANES : (column + 1) * LANES]
+
+
+def run_network(place, lanes, feats, weights):
+    atoms = feats[0].shape[0]
+    domains = len(feats)
+    quarters = 4
+    half_atoms = atoms // 2
+    width = ORB * LANES
+    rows = half_atoms // quarters * PAD
+    hidden = weights[0].shape[1]
+    vmem = pl.BlockSpec(memory_space=pltpu.VMEM)
+    return pl.pallas_call(
+        network_kernel,
+        grid=(domains, quarters),
+        out_shape=jax.ShapeDtypeStruct((domains, 2, half_atoms * PAD, width), BF16),
+        in_specs=[pl.BlockSpec(memory_space=pltpu.SMEM)] + [vmem] * (2 * domains + len(weights)),
+        out_specs=pl.BlockSpec((1, 2, rows, width), lambda d, q: (d, 0, q, 0)),
+        scratch_shapes=[
+            pltpu.VMEM((domains,) + lanes[0].shape, F32),
+            pltpu.VMEM((domains,) + lanes[0].shape[1:], F32),
+            pltpu.VMEM((domains, atoms, hidden), F32),
+            pltpu.VMEM((domains, atoms, hidden), F32),
+            pltpu.VMEM((domains * atoms, 2 * LANES), F32),
+            pltpu.VMEM((hidden, hidden), F32),
+        ],
+        compiler_params=pltpu.CompilerParams(vmem_limit_bytes=VMEM_LIMIT),
+        name="pair_network",
+    )(place, *lanes, *feats, *weights)
+
+
+def factor_panels(gram):
+    order = gram.shape[0]
+    count = order // PANEL
+    row = lax.broadcasted_iota(jnp.int32, (PANEL, order), 0)
+    lane = lax.broadcasted_iota(jnp.int32, (PANEL, order), 1)
+    work = [gram[q * PANEL : (q + 1) * PANEL] for q in range(count)]
+    extra = [jnp.where(lane == row + q * PANEL, 1.0, 0.0) for q in range(count)]
+    upper = []
+    inverse = []
+    for p in range(count):
+        base = p * PANEL
+        block = [jnp.broadcast_to(work[p][:, base + k : base + k + 1], (PANEL, order)) for k in range(PANEL)]
+        unit = [jnp.where(row == c, 1.0, 0.0) for c in range(PANEL)]
+        for r in range(PANEL):
+            pivot = spread_rows(block[r], r, PANEL)
+            root = lax.rsqrt(pivot)
+            column = jnp.where(row > r, block[r] * root, 0.0)
+            for k in range(r + 1, PANEL):
+                block[k] = block[k] - column * spread_rows(column, k, PANEL)
+            for c in range(r + 1):
+                lead = spread_rows(unit[c], r, PANEL) * root
+                unit[c] = jnp.where(row == r, lead, unit[c] - column * lead)
+        top = unit[0] * spread_rows(work[p], 0, PANEL)
+        side = unit[0] * spread_rows(extra[p], 0, PANEL)
+        for c in range(1, PANEL):
+            top = top + unit[c] * spread_rows(work[p], c, PANEL)
+            side = side + unit[c] * spread_rows(extra[p], c, PANEL)
+        top = jnp.where(lane >= row + base, top, 0.0)
+        upper.append(top)
+        inverse.append(side)
+        if p + 1 < count:
+            high = top.astype(BF16)
+            left = top - high.astype(F32)
+            middle = left.astype(BF16)
+            low = (left - middle.astype(F32)).astype(BF16)
+            both = jnp.concatenate([top, side], axis=1)
+            bhigh = both.astype(BF16)
+            bleft = both - bhigh.astype(F32)
+            bmiddle = bleft.astype(BF16)
+            blow = (bleft - bmiddle.astype(F32)).astype(BF16)
+            lhs = jnp.concatenate([high, high, middle, middle, high, low], axis=0)
+            rhs = jnp.concatenate([bhigh, bmiddle, bhigh, bmiddle, blow, bhigh], axis=0)
+            change = dot(lhs, rhs, TN)
+            for q in range(p + 1, count):
+                rows = slice(q * PANEL, (q + 1) * PANEL)
+                work[q] = work[q] - change[rows, :order]
+                extra[q] = extra[q] - change[rows, order:]
+    return jnp.concatenate(upper, axis=0), jnp.concatenate(inverse, axis=0)
+
+
+def lanczos_kernel(
+    place_ref,
+    x_own,
+    x_left1,
+    x_left2,
+    x_left3,
+    x_right1,
+    x_right2,
+    x_right3,
+    pairs_hbm,
+    alpha_ref,
+    beta_ref,
+    next_ref,
+    pairs,
+    xs,
+    ys,
+    qs,
+    flat,
+    turned,
+    sem,
+    rows_total,
+):
+    copy = pltpu.make_async_copy(pairs_hbm, pairs, sem)
+    copy.start()
+    place = place_ref[0]
+    atoms = x_own.shape[0]
+    half = atoms // 2
+    states = x_own.shape[2]
+    total = xs.shape[0]
+    atoms_all = total // PAD
+    chunk = 512
+    chunks = total // chunk
+    scale = 1.0 / rows_total
+
+    zero = jnp.zeros((PAD - ORB, states), F32)
+
+    def take(source, base):
+        for atom in range(source.shape[0]):
+            start = pl.multiple_of((base + atom) * PAD, PAD)
+            xs[pl.ds(start, ORB), :] = source[atom]
+            xs[pl.ds(start + ORB, PAD - ORB), :] = zero
+
+    take(x_own, place * atoms)
+    low = place_ref[1]
+    for step, (mine, other) in enumerate(
+        ((x_left1, x_right1), (x_left2, x_right2), (x_left3, x_right3)), 1
+    ):
+        base = (place ^ step) * atoms
+        take(mine, base + low * half)
+        take(other, base + (1 - low) * half)
+
+    def rows_of(ref, index):
+        return ref[pl.ds(pl.multiple_of(index * chunk, chunk), chunk), :]
+
+    def put(ref, index, value):
+        ref[pl.ds(pl.multiple_of(index * chunk, chunk), chunk), :] = value
+
+    def own_gram(pieces):
+        high, low_part = pieces
+        cross = dot(high, low_part, TN)
+        return dot(high, high, TN) + cross + jnp.transpose(cross)
+
+    def apply(ref):
+        for j in range(ORB):
+            flat_rows = slice(j * LANES, (j + 1) * LANES)
+            high, low_part = split(ref[pl.ds(j, atoms_all, stride=PAD), :])
+            flat[flat_rows, :states] = high
+            flat[flat_rows, states:] = low_part
+        for index in range(chunks):
+            high, low_part = split(rows_of(ref, index))
+            turned[:states, index * chunk : (index + 1) * chunk] = jnp.transpose(high)
+            turned[states:, index * chunk : (index + 1) * chunk] = jnp.transpose(low_part)
+
+        def forward(index, carry):
+            both = dot(rows_of(pairs, index), flat[...], NN)
+            put(ys, index, both[:, :states] + both[:, states:])
+            return carry
+
+        lax.fori_loop(0, chunks, forward, 0)
+        for j in range(ORB):
+            both = dot(turned[...], pairs[:, j * LANES : (j + 1) * LANES], NN)
+            back = jnp.transpose(both[:states] + both[states:])
+            ys[pl.ds(j, atoms_all, stride=PAD), :] = ys[pl.ds(j, atoms_all, stride=PAD), :] + back
+
+    def loop(function, results):
+        return lax.fori_loop(0, chunks, function, tuple(jnp.zeros((states, states), F32) for _ in range(results)))
+
+    def gram_start(index, carry):
+        return (carry[0] + own_gram(split(rows_of(xs, index))),)
+
+    (gram,) = loop(gram_start, 1)
+    factor, inverse = factor_panels(gram * scale)
+    copy.wait()
+    apply(xs)
+    inverse = split(inverse)
+
+    def first_alpha(index, carry):
+        current = dot_split(split(rows_of(xs, index)), inverse, NT)
+        residue = dot_split(split(rows_of(ys, index)), inverse, NT)
+        put(qs, index, current)
+        put(ys, index, residue)
+        return (carry[0] + dot_split(split(current), split(residue), TN),)
+
+    (alpha,) = loop(first_alpha, 1)
+    alpha = alpha * scale
+    alpha_ref[0] = alpha
+    alpha = split(alpha)
+
+    def first_gram(index, carry):
+        residue = rows_of(ys, index) - dot_split(split(rows_of(qs, index)), alpha, NN)
+        put(xs, index, residue)
+        return (carry[0] + own_gram(split(residue)),)
+
+    (gram,) = loop(first_gram, 1)
+    factor, inverse = factor_panels(gram * scale)
+    beta_ref[0] = factor
+    apply(xs)
+    inverse = split(inverse)
+    factor = split(factor)
+
+    def second_alpha(index, carry):
+        current = dot_split(split(rows_of(xs, index)), inverse, NT)
+        residue = dot_split(split(rows_of(ys, index)), inverse, NT)
+        residue = residue - dot_split(split(rows_of(qs, index)), factor, NT)
+        put(xs, index, current)
+        put(ys, index, residue)
+        return (carry[0] + dot_split(split(current), split(residue), TN),)
+
+    (alpha,) = loop(second_alpha, 1)
+    alpha = alpha * scale
+    alpha_ref[1] = alpha
+    alpha = split(alpha)
+
+    def second_gram(index, carry):
+        residue = rows_of(ys, index) - dot_split(split(rows_of(xs, index)), alpha, NN)
+        put(ys, index, residue)
+        return (carry[0] + own_gram(split(residue)),)
+
+    (gram,) = loop(second_gram, 1)
+    factor, inverse = factor_panels(gram * scale)
+    beta_ref[1] = factor
+    inverse = split(inverse)
+    mine = dot_split(split(rows_of(ys, place)), inverse, NT)
+    next_ref[...] = mine.reshape(atoms, PAD, states)[:, :ORB, :]
+
+
+def run_lanczos(place, own, left, right, pairs, rows_total):
+    atoms, _, states = own.shape
+    total = pairs.shape[0]
+    vmem = pl.BlockSpec(memory_space=pltpu.VMEM)
+
+    def kernel(*refs):
+        lanczos_kernel(*refs, rows_total)
+
+    return pl.pallas_call(
+        kernel,
+        out_shape=(
+            jax.ShapeDtypeStruct((STEPS, states, states), F32),
+            jax.ShapeDtypeStruct((STEPS, states, states), F32),
+            jax.ShapeDtypeStruct(own.shape, F32),
+        ),
+        in_specs=[pl.BlockSpec(memory_space=pltpu.SMEM)] + [vmem] * 7 + [pl.BlockSpec(memory_space=pl.ANY)],
+        out_specs=(vmem, vmem, vmem),
+        scratch_shapes=[
+            pltpu.VMEM(pairs.shape, BF16),
+            pltpu.VMEM((total, states), F32),
+            pltpu.VMEM((total, states), F32),
+            pltpu.VMEM((total, states), F32),
+            pltpu.VMEM((pairs.shape[1], 2 * states), BF16),
+            pltpu.VMEM((2 * states, total), BF16),
+            pltpu.SemaphoreType.DMA,
+        ],
+        compiler_params=pltpu.CompilerParams(vmem_limit_bytes=VMEM_LIMIT),
+        name="block_lanczos",
+    )(place, own, *left, *right, pairs)
+
+
+def exchange(shard, axis, mask):
+    devices = lax.axis_size(axis)
+    return lax.ppermute(shard, axis, [(i, i ^ mask) for i in range(devices)])
+
+
+def body(
+    node_feats,
+    distance,
+    neighbours,
+    counts,
+    w_source,
+    w_target,
+    w_radial,
+    w_middle,
+    w_output,
+    w_onsite,
+    initial,
+):
+    atoms_here, slots_here = neighbours.shape
+    domains = lax.axis_size("dom")
+    members = lax.axis_size("st") * lax.axis_size("sub")
+    atoms_all = atoms_here * domains
+    suits = (domains, atoms_all, 2 * members * slots_here, initial.shape[2]) == (4, LANES, LANES, LANES)
+    if not (suits and lax.axis_size("sub") == 2 and lax.axis_size("st") == 2):
+        return body_spread(
+            node_feats,
+            distance,
+            neighbours,
+            counts,
+            w_source,
+            w_target,
+            w_radial,
+            w_middle,
+            w_output,
+            w_onsite,
+            initial,
+        )
+    domain = lax.axis_index("dom")
+    core = lax.axis_index("sub")
+    member = lax.axis_index(("st", "sub"))
+    place = jnp.stack([domain, core]).astype(jnp.int32)
+
+    slot_index = member * slots_here + jnp.arange(slots_here, dtype=jnp.int32)
+    usable = slot_index[None, :] < counts[:, None]
+    named = jnp.where(usable, neighbours, -1).astype(F32)
+    own = jnp.stack([distance, named]).reshape(2, 2, atoms_here // 2, 1, slots_here)
+    own = jnp.where((jnp.arange(members) == member)[:, None], own, 0.0)
+    own = jnp.swapaxes(own, 1, 2).reshape(2, atoms_here // 2, LANES)
+    own = own + exchange(own, "sub", 1)
+    own = own + exchange(own, "st", 1)
+
+    lanes = [own] + [exchange(own, "dom", step) for step in range(1, domains)]
+    feats = [node_feats] + [exchange(node_feats, "dom", step) for step in range(1, domains)]
+    half = atoms_here // 2
+    part = lax.dynamic_slice_in_dim(initial, core * half, half, 0)
+    left = [exchange(part, "dom", step) for step in range(1, domains)]
+    right = [exchange(piece, "sub", 1) for piece in left]
+
+    def blocks_of(weights, order):
+        blocks = weights.reshape(-1, ORB, ORB).transpose(order)
+        return blocks
+
+    columns = jnp.pad(blocks_of(w_output, (2, 1, 0)), ((0, 0), (0, PAD - ORB), (0, 0)))
+    w_output_t = columns.reshape(ORB * PAD, -1)
+    spare = 2 * LANES - ORB * PAD
+
+    def onsite_weights(order):
+        blocks = jnp.pad(blocks_of(w_onsite, order), ((0, 0), (0, 0), (0, PAD - ORB)))
+        return jnp.pad(blocks.reshape(-1, ORB * PAD), ((0, 0), (0, spare)))
+
+    weights = (
+        w_source,
+        w_target,
+        w_radial,
+        w_middle.T,
+        w_output_t,
+        onsite_weights((0, 2, 1)),
+        onsite_weights((0, 1, 2)),
+    )
+    pairs = run_network(place, lanes, feats, weights)
+    pairs = pairs.reshape(atoms_all * PAD, ORB * LANES)
+    return run_lanczos(place, initial, left, right, pairs, float(atoms_all * ORB))
+
+
 def solution(mesh):
     placed = (
         P(("grp", "dom"), None),

time: 1620 us -> 105 us (0.06)
  local copies, waits for them, and re-layouts: 510 us -> 11.2 us
  matrix products: 428 us -> 0 us
  loops' own time: 293 us -> 0 us
  waiting for transfers between devices: 218 us -> 8.07 us
  other arithmetic: 129 us -> 1.47 us
  Pallas kernels: 0 us -> 64.2 us
    dynamic_slice x768 -> x1, local copies, waits for them, and re-layouts: 452 us -> 0.02 us  [body(): part = lax.dynamic_slice_in_dim(initial, core * half, half, 0)]
    dot_general x406 -> x0, matrix products: 428 us -> none  [the longest x384 393 us: row_step(): known = jnp.dot(factor_row, inverse, precision=lax.Precision.HIGHEST)]
    another operation x6 -> x0, loops' own time: 293 us -> none  [the longest x3 282 us: upper_factor(): lax.fori_loop(0, order, column_step, (matrix, jnp.zeros_like(matrix)))]
    psum x7 -> x0, waiting for transfers between devices: 218 us -> none  [the longest x5 154 us: totals(): return lax.psum(value, 'dom')]
    scatter-add x2 -> x0, other arithmetic: 80.4 us -> none  [edge_terms(): jax.ops.segment_sum(backward.reshape(-1, ORB, whole_rows.shape[-1]), loca...]
    pallas_call x0 -> x2, Pallas kernels: none -> 64.2 us  [the longest x1 46.5 us: run_lanczos(): pl.pallas_call(kernel, out_shape=(jax.ShapeDtypeStruct((STEPS, states, st...]
    sub x385 -> x0, other arithmetic: 32.6 us -> none  [the longest x384 31.5 us: column_step(): work = work - scaled[:, None] * scaled[None, :]]
    dynamic_update_slice x768 -> x0, local copies, waits for them, and re-layouts: 26.1 us -> none  [the longest x384 14.3 us: column_step(): lax.dynamic_update_slice_in_dim(lower, scaled[:, None], column_index, 1)]
  transfers between devices with their start and end apart: 12 -> 14, of which waited for: 7 -> 4; matrix products, arithmetic and copies ran while one was open for 8% -> 7% of each run, Pallas kernels for 0% -> 17%
where the time goes in v1:
time: 105 us; the launch traced here: 103 us
  Pallas kernels  64.2 us (61%)
  starting transfers between devices  17.5 us (17%)
  local copies, waits for them, and re-layouts  11.2 us (11%)
  waiting for transfers between devices  8.07 us (8%)
  other arithmetic  1.47 us (1%)
    pallas_call x1, Pallas kernels, run_lanczos(): pl.pallas_call(kernel, out_shape=(jax.ShapeDtypeStruct((STEPS, states, st...  46.5 us
    pallas_call x1, Pallas kernels, run_network(): pl.pallas_call(network_kernel, grid=(domains, quarters), out_shape=jax.Sh...  17.7 us
    ppermute x14, starting transfers between devices, exchange(): return lax.ppermute(shard, axis, [(i, i ^ mask) for i in range(devices)])  17.5 us
    ppermute x14, waiting for transfers between devices, exchange(): return lax.ppermute(shard, axis, [(i, i ^ mask) for i in range(devices)])  8.07 us
    unnamed x31, local copies, waits for them, and re-layouts  4.05 us
  transfers between devices with their start and end apart: 14, of which 4 were waited for; matrix products, arithmetic and copies ran while one was open for 7% of the time, Pallas kernels for 17%

profile of v1, /device:TPU:0, one launch (start us, length us, event | category | flops | bytes accessed | tf_op | source)
XLA Modules:
  0.0 103.4 jit_solution(17348300423461260757)
XLA Ops:
  0.7 0.8 select_convert_fusion
  1.4 0.1 stack.22
  1.5 0.8 stack.21
  2.3 0.1 copy.32
  2.4 0.1 broadcast_in_dim.44
  2.6 0.1 broadcast_in_dim.37
  2.6 0.1 broadcast_in_dim.38
  2.7 0.5 collective-permute-start.6
  3.3 1.1 %copy.38.refs_1_ = f32[32,13,128]{2,1,0:T(8,128)S(1)} copy(f32[32,13,128]{2,0,1:T(8,128)} %param.21) | data formatting | bytes 425984 | tf_op args[10]
  4.4 2.7 %collective-permute-start = (f32[16,13,128]{2,1,0:T(8,128)S(1)}, f32[16,13,128]{2,1,0:T(8,128)S(1)}, u32[]{:S(2)}, u32[]{:S(2)}) collective-permute-start(f32[16,13,128]{2,1,0:T(8,128)S(1)} %constant_dynamic-slice_fusion), channel_id=1, source_target_pairs={{0,4},{4,0},{8,12},{12,8},{1,5},{5,1},{9,13},{13,9},{2,6},{6,2},{1... | collective-permute-start | bytes 319496 | tf_op jit(solution)/shard_map/ppermute | solution.py:600
  7.0 2.6 %collective-permute-start.1 = (f32[16,13,128]{2,1,0:T(8,128)S(1)}, f32[16,13,128]{2,1,0:T(8,128)S(1)}, u32[]{:S(2)}, u32[]{:S(2)}) collective-permute-start(f32[16,13,128]{2,1,0:T(8,128)S(1)} %constant_dynamic-slice_fusion), channel_id=1, source_target_pairs={{0,8},{4,12},{8,0},{12,4},{1,9},{5,13},{9,1},{13,5},{2,10},{6,14},... | collective-permute-start | bytes 319496 | tf_op jit(solution)/shard_map/ppermute | solution.py:600
  9.6 0.0 collective-permute-start.2
  9.6 0.0 collective-permute-done.6
  9.6 1.8 %collective-permute-start.7 = (f32[2,16,128]{2,1,0:T(8,128)S(1)}, f32[2,16,128]{2,1,0:T(8,128)S(1)}, u32[]{:S(2)}, u32[]{:S(2)}) collective-permute-start(f32[2,16,128]{2,1,0:T(8,128)S(1)} %fusion), channel_id=1, source_target_pairs={{0,2},{2,0},{1,3},{3,1},{4,6},{6,4},{5,7},{7,5},{8,10},{10,8},{9,1... | collective-permute-start | bytes 49160 | tf_op jit(solution)/shard_map/ppermute | solution.py:600
  11.4 0.7 collective-permute-start.11
  12.1 1.4 %collective-permute-done.7 = f32[2,16,128]{2,1,0:T(8,128)S(1)} collective-permute-done((f32[2,16,128]{2,1,0:T(8,128)S(1)}, f32[2,16,128]{2,1,0:T(8,128)S(1)}, u32[]{:S(2)}, u32[]{:S(2)}) %collective-permute-start.7) | collective-permute-done | bytes 16416 | tf_op jit(solution)/shard_map/ppermute | solution.py:600
  13.4 2.1 %collective-permute-start.12 = (bf16[32,256]{1,0:T(8,128)(2,1)}, bf16[32,256]{1,0:T(8,128)(2,1)S(1)}, u32[]{:S(2)}, u32[]{:S(2)}) collective-permute-start(bf16[32,256]{1,0:T(8,128)(2,1)} %feat0.1), channel_id=1, source_target_pairs={{0,8},{4,12},{8,0},{12,4},{1,9},{5,13},{9,1},{13,5},{2,10},{6,14},... | collective-permute-start | bytes 49160 | tf_op jit(solution)/shard_map/ppermute | solution.py:600
  15.6 1.0 %collective-permute-done.11.feat1 = bf16[32,256]{1,0:T(8,128)(2,1)S(1)} collective-permute-done((bf16[32,256]{1,0:T(8,128)(2,1)}, bf16[32,256]{1,0:T(8,128)(2,1)S(1)}, u32[]{:S(2)}, u32[]{:S(2)}) %collective-permute-start.11) | collective-permute-done | bytes 16416 | tf_op jit(solution)/shard_map/ppermute | solution.py:600
  16.6 4.0 %collective-permute-start.13 = (bf16[32,256]{1,0:T(8,128)(2,1)}, bf16[32,256]{1,0:T(8,128)(2,1)S(1)}, u32[]{:S(2)}, u32[]{:S(2)}) collective-permute-start(bf16[32,256]{1,0:T(8,128)(2,1)} %feat0.1), channel_id=1, source_target_pairs={{0,12},{4,8},{8,4},{12,0},{1,13},{5,9},{9,5},{13,1},{2,14},{6,10},... | collective-permute-start | bytes 49160 | tf_op jit(solution)/shard_map/ppermute | solution.py:600
  20.7 2.6 %collective-permute-done.12.feat2 = bf16[32,256]{1,0:T(8,128)(2,1)S(1)} collective-permute-done((bf16[32,256]{1,0:T(8,128)(2,1)}, bf16[32,256]{1,0:T(8,128)(2,1)S(1)}, u32[]{:S(2)}, u32[]{:S(2)}) %collective-permute-start.12) | collective-permute-done | bytes 16416 | tf_op jit(solution)/shard_map/ppermute | solution.py:600
  23.2 2.4 %collective-permute-start.10 = (f32[2,16,128]{2,1,0:T(8,128)S(1)}, f32[2,16,128]{2,1,0:T(8,128)S(1)}, u32[]{:S(2)}, u32[]{:S(2)}) collective-permute-start(f32[2,16,128]{2,1,0:T(8,128)S(1)} %add.37.lane0), channel_id=1, source_target_pairs={{0,12},{4,8},{8,4},{12,0},{1,13},{5,9},{9,5},{13,1},{2,14},{6,10},... | collective-permute-start | bytes 49160 | tf_op jit(solution)/shard_map/ppermute | solution.py:600
  25.7 0.0 collective-permute-done.13.feat3
  25.7 0.0 collective-permute-start.8
  25.7 3.1 %collective-permute-done.10.lane3 = f32[2,16,128]{2,1,0:T(8,128)S(1)} collective-permute-done((f32[2,16,128]{2,1,0:T(8,128)S(1)}, f32[2,16,128]{2,1,0:T(8,128)S(1)}, u32[]{:S(2)}, u32[]{:S(2)}) %collective-permute-start.10) | collective-permute-done | bytes 16416 | tf_op jit(solution)/shard_map/ppermute | solution.py:600
  28.8 0.0 copy-start.1
  28.8 0.1 collective-permute-start.3
  28.9 0.5 collective-permute-start.4
  29.4 0.1 collective-permute-start.5
  29.5 0.7 pad_add_fusion.place_ref.refs_0_
  30.1 0.9 reshape.40
  31.1 0.1 copy.36
  31.2 0.7 pad.20.w_onsite_a
  31.9 0.1 copy.37
  32.0 0.7 pad.22.w_onsite_b
  32.7 0.9 reshape.38
  33.7 0.6 pad.18
  34.3 1.7 %copy.33 = bf16[256,256]{0,1:T(8,128)(2,1)} copy(bf16[256,256]{1,0:T(8,128)(2,1)} %param.18) | data formatting | bytes 262144 | tf_op args[7]
  36.0 0.0 collective-permute-done.8.lane1
  36.0 0.0 collective-permute-done.9.lane2
  36.1 0.5 copy-done.12
  36.6 0.0 copy-done.13
  36.6 17.7 %pair_network.1 = bf16[4,2,256,1664]{3,2,1,0:T(8,128)(2,1)} custom-call(s32[2]{0:T(128)} %pad_add_fusion.place_ref.refs_0_, f32[2,16,128]{2,1,0:T(8,128)} %copy-done.7, f32[2,16,128]{2,1,0:T(8,128)} %copy-done.12, f32[2,16,128]{2,1,0:T(8,128)} %copy-done.13, f32[2,16,128]{2,1,0:T(8,128)} %copy-done.11, bf16[32,256]{1,0:T(8,128)(2,1)} %feat0.1, ...), custom_call_target="tpu_custom_call" | custom-call | tf_op jit(solution)/shard_map/pair_network/pallas_call | solution.py:352
  54.4 0.0 collective-permute-done.4.refs_6_
  54.4 0.6 copy-done.4
  55.0 0.1 copy-done.5
  55.1 0.1 copy-done.6
  55.1 46.5 %block_lanczos.1 = (f32[2,128,128]{2,1,0:T(8,128)}, f32[2,128,128]{2,1,0:T(8,128)}, f32[32,13,128]{2,1,0:T(8,128)}) custom-call(s32[2]{0:T(128)} %pad_add_fusion.place_ref.refs_0_, f32[32,13,128]{2,1,0:T(8,128)} %copy-done, f32[16,13,128]{2,1,0:T(8,128)} %copy-done.1, f32[16,13,128]{2,1,0:T(8,128)} %copy-done.2, f32[16,13,128]{2,1,0:T(8,128)} %copy-done.3, ...), custom_call_target="tpu_custom_call" | custom-call | tf_op jit(solution)/shard_map/block_lanczos/pallas_call | solution.py:575
  101.7 1.7 %copy.39 = f32[32,13,128]{2,0,1:T(8,128)} copy(f32[32,13,128]{2,1,0:T(8,128)} %get-tuple-element.11) | data formatting | bytes 425984 | tf_op jit(solution)/shard_map/block_lanczos/pallas_call | solution.py:575
  (40 shorter events, 0.2 us)
Async XLA Ops:
  2.7 6.9 %collective-permute-start.6 = (f32[2,16,128]{2,1,0:T(8,128)S(1)}, f32[2,16,128]{2,1,0:T(8,128)S(1)}, u32[]{:S(2)}, u32[]{:S(2)}) collective-permute-start(f32[2,16,128]{2,1,0:T(8,128)S(1)} %broadcast_select_fusion), channel_id=1, source_target_pairs={{0,1},{1,0},{2,3},{3,2},{4,5},{5,4},{6,7},{7,6},{8,9},{9,8},{10,11... | collective-permute-start | bytes 49160 | tf_op jit(solution)/shard_map/ppermute | solution.py:600
  4.3 50.1 %copy-start = (f32[32,13,128]{2,1,0:T(8,128)}, f32[32,13,128]{2,1,0:T(8,128)S(1)}, u32[]{:S(2)}) copy-start(f32[32,13,128]{2,1,0:T(8,128)S(1)} %copy.38.refs_1_) | copy-start | bytes 638980
  4.4 24.4 %collective-permute-start = (f32[16,13,128]{2,1,0:T(8,128)S(1)}, f32[16,13,128]{2,1,0:T(8,128)S(1)}, u32[]{:S(2)}, u32[]{:S(2)}) collective-permute-start(f32[16,13,128]{2,1,0:T(8,128)S(1)} %constant_dynamic-slice_fusion), channel_id=1, source_target_pairs={{0,4},{4,0},{8,12},{12,8},{1,5},{5,1},{9,13},{13,9},{2,6},{6,2},{1... | collective-permute-start | bytes 319496 | tf_op jit(solution)/shard_map/ppermute | solution.py:600
  7.0 21.9 %collective-permute-start.1 = (f32[16,13,128]{2,1,0:T(8,128)S(1)}, f32[16,13,128]{2,1,0:T(8,128)S(1)}, u32[]{:S(2)}, u32[]{:S(2)}) collective-permute-start(f32[16,13,128]{2,1,0:T(8,128)S(1)} %constant_dynamic-slice_fusion), channel_id=1, source_target_pairs={{0,8},{4,12},{8,0},{12,4},{1,9},{5,13},{9,1},{13,5},{2,10},{6,14},... | collective-permute-start | bytes 319496 | tf_op jit(solution)/shard_map/ppermute | solution.py:600
  9.6 19.8 %collective-permute-start.2 = (f32[16,13,128]{2,1,0:T(8,128)S(1)}, f32[16,13,128]{2,1,0:T(8,128)S(1)}, u32[]{:S(2)}, u32[]{:S(2)}) collective-permute-start(f32[16,13,128]{2,1,0:T(8,128)S(1)} %constant_dynamic-slice_fusion), channel_id=1, source_target_pairs={{0,12},{4,8},{8,4},{12,0},{1,13},{5,9},{9,5},{13,1},{2,14},{6,10},... | collective-permute-start | bytes 319496 | tf_op jit(solution)/shard_map/ppermute | solution.py:600
  9.6 3.8 %collective-permute-start.7 = (f32[2,16,128]{2,1,0:T(8,128)S(1)}, f32[2,16,128]{2,1,0:T(8,128)S(1)}, u32[]{:S(2)}, u32[]{:S(2)}) collective-permute-start(f32[2,16,128]{2,1,0:T(8,128)S(1)} %fusion), channel_id=1, source_target_pairs={{0,2},{2,0},{1,3},{3,1},{4,6},{6,4},{5,7},{7,5},{8,10},{10,8},{9,1... | collective-permute-start | bytes 49160 | tf_op jit(solution)/shard_map/ppermute | solution.py:600
  11.4 5.2 %collective-permute-start.11 = (bf16[32,256]{1,0:T(8,128)(2,1)}, bf16[32,256]{1,0:T(8,128)(2,1)S(1)}, u32[]{:S(2)}, u32[]{:S(2)}) collective-permute-start(bf16[32,256]{1,0:T(8,128)(2,1)} %feat0.1), channel_id=1, source_target_pairs={{0,4},{4,0},{8,12},{12,8},{1,5},{5,1},{9,13},{13,9},{2,6},{6,2},{1... | collective-permute-start | bytes 49160 | tf_op jit(solution)/shard_map/ppermute | solution.py:600
  13.4 9.8 %collective-permute-start.12 = (bf16[32,256]{1,0:T(8,128)(2,1)}, bf16[32,256]{1,0:T(8,128)(2,1)S(1)}, u32[]{:S(2)}, u32[]{:S(2)}) collective-permute-start(bf16[32,256]{1,0:T(8,128)(2,1)} %feat0.1), channel_id=1, source_target_pairs={{0,8},{4,12},{8,0},{12,4},{1,9},{5,13},{9,1},{13,5},{2,10},{6,14},... | collective-permute-start | bytes 49160 | tf_op jit(solution)/shard_map/ppermute | solution.py:600
  15.6 20.5 %copy-start.7 = (f32[2,16,128]{2,1,0:T(8,128)}, f32[2,16,128]{2,1,0:T(8,128)S(1)}, u32[]{:S(2)}) copy-start(f32[2,16,128]{2,1,0:T(8,128)S(1)} %add.37.lane0) | copy-start | bytes 49156
  16.6 19.4 %copy-start.8 = (bf16[32,256]{1,0:T(8,128)(2,1)}, bf16[32,256]{1,0:T(8,128)(2,1)S(1)}, u32[]{:S(2)}) copy-start(bf16[32,256]{1,0:T(8,128)(2,1)S(1)} %collective-permute-done.11.feat1) | copy-start | bytes 49156
  16.6 9.1 %collective-permute-start.13 = (bf16[32,256]{1,0:T(8,128)(2,1)}, bf16[32,256]{1,0:T(8,128)(2,1)S(1)}, u32[]{:S(2)}, u32[]{:S(2)}) collective-permute-start(bf16[32,256]{1,0:T(8,128)(2,1)} %feat0.1), channel_id=1, source_target_pairs={{0,12},{4,8},{8,4},{12,0},{1,13},{5,9},{9,5},{13,1},{2,14},{6,10},... | collective-permute-start | bytes 49160 | tf_op jit(solution)/shard_map/ppermute | solution.py:600
  23.2 12.8 %copy-start.9 = (bf16[32,256]{1,0:T(8,128)(2,1)}, bf16[32,256]{1,0:T(8,128)(2,1)S(1)}, u32[]{:S(2)}) copy-start(bf16[32,256]{1,0:T(8,128)(2,1)S(1)} %collective-permute-done.12.feat2) | copy-start | bytes 49156
  23.2 5.5 %collective-permute-start.10 = (f32[2,16,128]{2,1,0:T(8,128)S(1)}, f32[2,16,128]{2,1,0:T(8,128)S(1)}, u32[]{:S(2)}, u32[]{:S(2)}) collective-permute-start(f32[2,16,128]{2,1,0:T(8,128)S(1)} %add.37.lane0), channel_id=1, source_target_pairs={{0,12},{4,8},{8,4},{12,0},{1,13},{5,9},{9,5},{13,1},{2,14},{6,10},... | collective-permute-start | bytes 49160 | tf_op jit(solution)/shard_map/ppermute | solution.py:600
  25.7 10.4 %copy-start.10 = (bf16[32,256]{1,0:T(8,128)(2,1)}, bf16[32,256]{1,0:T(8,128)(2,1)S(1)}, u32[]{:S(2)}) copy-start(bf16[32,256]{1,0:T(8,128)(2,1)S(1)} %collective-permute-done.13.feat3) | copy-start | bytes 49156
  25.7 10.3 %collective-permute-start.8 = (f32[2,16,128]{2,1,0:T(8,128)S(1)}, f32[2,16,128]{2,1,0:T(8,128)S(1)}, u32[]{:S(2)}, u32[]{:S(2)}) collective-permute-start(f32[2,16,128]{2,1,0:T(8,128)S(1)} %add.37.lane0), channel_id=1, source_target_pairs={{0,4},{4,0},{8,12},{12,8},{1,5},{5,1},{9,13},{13,9},{2,6},{6,2},{1... | collective-permute-start | bytes 49160 | tf_op jit(solution)/shard_map/ppermute | solution.py:600
  28.8 7.3 %copy-start.11 = (f32[2,16,128]{2,1,0:T(8,128)}, f32[2,16,128]{2,1,0:T(8,128)S(1)}, u32[]{:S(2)}) copy-start(f32[2,16,128]{2,1,0:T(8,128)S(1)} %collective-permute-done.10.lane3) | copy-start | bytes 49156
  28.8 7.2 %collective-permute-start.9 = (f32[2,16,128]{2,1,0:T(8,128)S(1)}, f32[2,16,128]{2,1,0:T(8,128)S(1)}, u32[]{:S(2)}, u32[]{:S(2)}) collective-permute-start(f32[2,16,128]{2,1,0:T(8,128)S(1)} %add.37.lane0), channel_id=1, source_target_pairs={{0,8},{4,12},{8,0},{12,4},{1,9},{5,13},{9,1},{13,5},{2,10},{6,14},... | collective-permute-start | bytes 49160 | tf_op jit(solution)/shard_map/ppermute | solution.py:600
  28.8 25.6 %copy-start.1 = (f32[16,13,128]{2,1,0:T(8,128)}, f32[16,13,128]{2,1,0:T(8,128)S(1)}, u32[]{:S(2)}) copy-start(f32[16,13,128]{2,1,0:T(8,128)S(1)} %collective-permute-done.refs_2_) | copy-start | bytes 319492
  28.8 25.6 %collective-permute-start.3 = (f32[16,13,128]{2,1,0:T(8,128)S(1)}, f32[16,13,128]{2,1,0:T(8,128)S(1)}, u32[]{:S(2)}, u32[]{:S(2)}) collective-permute-start(f32[16,13,128]{2,1,0:T(8,128)S(1)} %collective-permute-done.refs_2_), channel_id=1, source_target_pairs={{0,1},{1,0},{2,3},{3,2},{4,5},{5,4},{6,7},{7,6},{8,9},{9,8},{10,11... | collective-permute-start | bytes 319496 | tf_op jit(solution)/shard_map/ppermute | solution.py:600
  28.9 25.5 %copy-start.2 = (f32[16,13,128]{2,1,0:T(8,128)}, f32[16,13,128]{2,1,0:T(8,128)S(1)}, u32[]{:S(2)}) copy-start(f32[16,13,128]{2,1,0:T(8,128)S(1)} %collective-permute-done.1.refs_3_) | copy-start | bytes 319492
  28.9 25.5 %collective-permute-start.4 = (f32[16,13,128]{2,1,0:T(8,128)S(1)}, f32[16,13,128]{2,1,0:T(8,128)S(1)}, u32[]{:S(2)}, u32[]{:S(2)}) collective-permute-start(f32[16,13,128]{2,1,0:T(8,128)S(1)} %collective-permute-done.1.refs_3_), channel_id=1, source_target_pairs={{0,1},{1,0},{2,3},{3,2},{4,5},{5,4},{6,7},{7,6},{8,9},{9,8},{10,11... | collective-permute-start | bytes 319496 | tf_op jit(solution)/shard_map/ppermute | solution.py:600
  29.4 25.1 %copy-start.3 = (f32[16,13,128]{2,1,0:T(8,128)}, f32[16,13,128]{2,1,0:T(8,128)S(1)}, u32[]{:S(2)}) copy-start(f32[16,13,128]{2,1,0:T(8,128)S(1)} %collective-permute-done.2.refs_4_) | copy-start | bytes 319492
  29.4 25.0 %collective-permute-start.5 = (f32[16,13,128]{2,1,0:T(8,128)S(1)}, f32[16,13,128]{2,1,0:T(8,128)S(1)}, u32[]{:S(2)}, u32[]{:S(2)}) collective-permute-start(f32[16,13,128]{2,1,0:T(8,128)S(1)} %collective-permute-done.2.refs_4_), channel_id=1, source_target_pairs={{0,1},{1,0},{2,3},{3,2},{4,5},{5,4},{6,7},{7,6},{8,9},{9,8},{10,11... | collective-permute-start | bytes 319496 | tf_op jit(solution)/shard_map/ppermute | solution.py:600
  36.0 0.6 copy-start.12
  36.0 0.6 copy-start.13
  54.4 0.7 copy-start.4
  54.4 0.7 copy-start.5
  54.4 0.8 copy-start.6

commit v2 on v0

--- a/solution.py
+++ b/solution.py
@@ -1,6 +1,8 @@
 import jax
 import jax.numpy as jnp
 from jax import lax
+from jax.experimental import pallas as pl
+from jax.experimental.pallas import tpu as pltpu
 from jax.sharding import PartitionSpec as P
 
 ORB = 13
@@ -119,7 +121,7 @@
     return (jnp.stack(alpha_list), jnp.stack(beta_list), current)
 
 
-def body(
+def body_spread(
     node_feats,
     distance,
     neighbours,
@@ -179,6 +181,536 @@
     return (alpha_blocks, beta_blocks, final_rows)
 
 
+F32 = jnp.float32
+BF16 = jnp.bfloat16
+LANES = 128
+PAD = 16
+PANEL = 8
+NEAR = 3
+VMEM_LIMIT = 56 * 1024 * 1024
+
+
+def dims(left, right):
+    return (((left,), (right,)), ((), ()))
+
+
+def dot(left, right, contract):
+    return lax.dot_general(left, right, contract, preferred_element_type=F32)
+
+
+def split(value):
+    high = value.astype(BF16)
+    return high, (value - high.astype(F32)).astype(BF16)
+
+
+def dot_split(left, right, contract):
+    lh, ll = left
+    rh, rl = right
+    return dot(lh, rh, contract) + (dot(ll, rh, contract) + dot(lh, rl, contract))
+
+
+NN = dims(1, 0)
+NT = dims(1, 1)
+TN = dims(0, 0)
+
+
+def silu(value):
+    half = 0.5 * value
+    return half + half * jnp.tanh(half)
+
+
+def spread_rows(value, row, count):
+    return jnp.broadcast_to(value[row : row + 1, :], (count, value.shape[1]))
+
+
+def lanes_kernel(place_ref, distance, named, counts, out_ref):
+    slots, atoms = distance.shape
+    member = place_ref[2]
+    slot = lax.broadcasted_iota(jnp.int32, (slots, atoms), 0) + member * slots
+    usable = slot < counts[...]
+    names = jnp.where(usable, named[...], -1).astype(F32)
+    turned = jnp.transpose(jnp.concatenate([distance[...], names], axis=0))
+    group = atoms // 4
+    space = jnp.zeros((2 * group, LANES // 2 - slots), F32)
+    for kind in range(2):
+        part = turned[:, kind * slots : (kind + 1) * slots]
+        first = jnp.concatenate([part[:group], part[2 * group : 3 * group]], axis=0)
+        second = jnp.concatenate([part[group : 2 * group], part[3 * group :]], axis=0)
+        row = jnp.concatenate([first, space, second, space], axis=1)
+        out_ref[kind] = pltpu.roll(row, member * slots, 1)
+
+
+def run_lanes(place, distance, named, counts):
+    vmem = pl.BlockSpec(memory_space=pltpu.VMEM)
+    return pl.pallas_call(
+        lanes_kernel,
+        out_shape=jax.ShapeDtypeStruct((2, distance.shape[1] // 2, LANES), F32),
+        in_specs=[pl.BlockSpec(memory_space=pltpu.SMEM), vmem, vmem, vmem],
+        out_specs=vmem,
+        name="slot_lanes",
+    )(place, distance, named, counts)
+
+
+def network_kernel(
+    place_ref,
+    pack0,
+    pack1,
+    pack2,
+    pack3,
+    w_source,
+    w_target,
+    w_radial,
+    w_middle,
+    w_output_t,
+    w_onsite_t,
+    out_ref,
+    pairs,
+    envelopes,
+    source,
+    target,
+    onsite,
+    feats,
+    mixer,
+    middle,
+    outer,
+    raw,
+    rows,
+    placed_ref,
+):
+    domain = pl.program_id(0)
+    group = pl.program_id(1)
+    domains = 4
+    groups = pl.num_programs(1)
+    atoms = source.shape[1]
+    tiles = atoms // 4
+    basis = w_radial.shape[0]
+    stride = ORB * PAD
+
+    @pl.when((domain == 0) & (group == 0))
+    def prepare():
+        place = place_ref[0]
+        for step, pack in enumerate((pack0, pack1, pack2, pack3)):
+            where = place ^ step
+            reach = pack[: 2 * tiles]
+            pairs[where, 0] = reach
+            pairs[where, 1] = pack[2 * tiles : 4 * tiles]
+            envelopes[where] = 0.5 * (jnp.cos(jnp.pi * reach / RADIUS) + 1.0)
+            got = jnp.concatenate([pack[4 * tiles : 4 * tiles + atoms], pack[4 * tiles + atoms :]], axis=1)
+            got = got.astype(BF16)
+            source[where] = dot(got, w_source[...], NN)
+            target[where] = dot(got, w_target[...], NN)
+            feats[where] = got
+        middle[...] = jnp.transpose(w_middle[...].astype(F32)).astype(BF16)
+        empty = jnp.zeros((PAD - ORB, rows.shape[1]), F32)
+
+        def fill_raw(weights):
+            for side in range(raw.shape[0]):
+                raw[side] = weights[:, side * LANES : (side + 1) * LANES].astype(F32)
+
+        def read_raw(where):
+            return jnp.concatenate([raw[side, where, :] for side in range(raw.shape[0])], axis=1)
+
+        def arrange(read):
+            for j in range(ORB):
+                rows[j * PAD : j * PAD + ORB, :] = read(j)
+                rows[j * PAD + ORB : (j + 1) * PAD, :] = empty
+            return rows[...].astype(BF16)
+
+        whole = feats[...].reshape(domains * atoms, feats.shape[2])
+        fill_raw(w_onsite_t)
+        first = dot(arrange(lambda j: read_raw(pl.ds(j, ORB, stride=ORB))), whole, NT)
+        second = dot(arrange(lambda j: read_raw(pl.ds(j * ORB, ORB))), whole, NT)
+        onsite[...] = 0.5 * (0.5 * (first + second)).astype(BF16).astype(F32)
+        fill_raw(w_output_t)
+        outer[...] = arrange(lambda j: read_raw(pl.ds(j, ORB, stride=ORB)))
+
+    @pl.when(group == 0)
+    def mix():
+        following = lax.rem(domain + 1, domains)
+        spare = mixer.shape[1] - basis - 3 * atoms
+        stacked = jnp.concatenate(
+            [
+                w_radial[...].astype(F32),
+                target[domain],
+                target[following],
+                source[domain],
+                jnp.zeros((spare, mixer.shape[0]), F32),
+            ],
+            axis=0,
+        )
+        mixer[...] = jnp.transpose(stacked).astype(BF16)
+
+    lane = lax.broadcasted_iota(jnp.int32, (1, LANES), 1)
+    upper = lane >= LANES // 2
+    row2 = lax.broadcasted_iota(jnp.int32, (LANES, LANES), 0)
+    column2 = lax.broadcasted_iota(jnp.int32, (LANES, LANES), 1)
+    centres = RADIUS * row2.astype(F32) / basis
+    scale = 1.0 / (2.0 * RADIUS / basis)
+    inputs = []
+    envs = []
+    names = []
+    for u in range(tiles):
+        line = pl.ds(group * tiles + u, 1)
+        reach = pairs[domain, 0, line, :]
+        name = pairs[domain, 1, line, :].astype(jnp.int32)
+        envs.append(envelopes[domain, line, :])
+        names.append(name)
+        radial_t = jnp.exp(-jnp.square((reach - centres) * scale))
+        local = lax.rem(name - domain * atoms + domains * atoms, domains * atoms)
+        who = group * 2 * tiles + u + jnp.where(upper, tiles, 0)
+        near = row2[: 2 * atoms] == local
+        mine = row2[: 2 * atoms] == who
+        inputs.append(
+            jnp.concatenate(
+                [radial_t, jnp.where(near, 1.0, 0.0), jnp.where(mine, 1.0, 0.0)], axis=0
+            ).astype(BF16)
+        )
+    columns = jnp.concatenate(inputs, axis=1)
+    hidden = silu(dot(mixer[...], columns, NN)).astype(BF16)
+    second = silu(dot(middle[...], hidden, NN)).astype(BF16)
+    blocks = dot(outer[...], second, NN)
+    flags = jnp.concatenate(
+        [jnp.where(column2 < LANES // 2, row2, -2), jnp.where(column2 < LANES // 2, -2, row2)], axis=0
+    )
+    for u in range(tiles):
+        piece = (blocks[:, u * LANES : (u + 1) * LANES] * envs[u]).astype(BF16)
+        chosen = jnp.where(flags == names[u], 1.0, 0.0).astype(BF16)
+        placed = dot(piece, chosen, NT)
+        for h in range(2):
+            place = h * tiles + u
+            atom = domain * atoms + group * 2 * tiles + place
+            whole = placed[:, h * LANES : (h + 1) * LANES] + jnp.where(lane == atom, onsite[...], 0.0)
+            rows_at = slice(place * stride, (place + 1) * stride)
+            placed_ref[rows_at, :] = whole
+    for j in range(ORB):
+        for i in range(ORB):
+            tile = placed_ref[pl.ds(j * PAD + i, 2 * tiles, stride=stride), :]
+            out_ref[i, :, j * LANES : (j + 1) * LANES] = tile.astype(BF16)
+
+
+def run_network(place, packs, weights):
+    domains = len(packs)
+    atoms = packs[0].shape[0] // 3
+    groups = 2
+    width = ORB * LANES
+    tiles = atoms // 4
+    hidden = weights[0].shape[1]
+    vmem = pl.BlockSpec(memory_space=pltpu.VMEM)
+    return pl.pallas_call(
+        network_kernel,
+        grid=(domains, groups),
+        out_shape=jax.ShapeDtypeStruct((ORB, domains * atoms, width), BF16),
+        in_specs=[pl.BlockSpec(memory_space=pltpu.SMEM)] + [vmem] * (domains + len(weights)),
+        out_specs=pl.BlockSpec((ORB, 2 * tiles, width), lambda d, g: (0, groups * d + g, 0)),
+        scratch_shapes=[
+            pltpu.VMEM((domains, 2, 2 * tiles, LANES), F32),
+            pltpu.VMEM((domains, 2 * tiles, LANES), F32),
+            pltpu.VMEM((domains, atoms, hidden), F32),
+            pltpu.VMEM((domains, atoms, hidden), F32),
+            pltpu.VMEM((ORB * PAD, LANES), F32),
+            pltpu.VMEM((domains, atoms, weights[0].shape[0]), BF16),
+            pltpu.VMEM((hidden, hidden), BF16),
+            pltpu.VMEM((hidden, hidden), BF16),
+            pltpu.VMEM((ORB * PAD, hidden), BF16),
+            pltpu.VMEM((hidden // LANES, ORB * ORB, LANES), F32),
+            pltpu.VMEM((ORB * PAD, hidden), F32),
+            pltpu.VMEM((2 * tiles * ORB * PAD, LANES), F32),
+        ],
+        compiler_params=pltpu.CompilerParams(vmem_limit_bytes=VMEM_LIMIT),
+        cost_estimate=pl.CostEstimate(flops=6_000_000_000, bytes_accessed=8_000_000, transcendentals=6_000_000),
+        name="pair_network",
+    )(place, *packs, *weights)
+
+
+def column_of(value, lane):
+    return jnp.broadcast_to(value[:, lane : lane + 1], (value.shape[0], LANES))
+
+
+def split_three(value):
+    high = value.astype(BF16)
+    rest = value - high.astype(F32)
+    middle = rest.astype(BF16)
+    return high, middle, (rest - middle.astype(F32)).astype(BF16)
+
+
+def outer_change(top, side):
+    high, middle, low = split_three(top)
+    sides = split_three(side)
+    wide = [jnp.concatenate([t, s], axis=1) for t, s in zip((high, middle, low), sides)]
+    left = jnp.concatenate([high, high, middle, middle, high, low], axis=0)
+    right = jnp.concatenate([wide[0], wide[1], wide[0], wide[1], wide[2], wide[0]], axis=0)
+    return dot(left, right, TN)
+
+
+def factor_panels(gram, fill=()):
+    order = gram.shape[0]
+    count = order // PANEL
+    row = lax.broadcasted_iota(jnp.int32, (PANEL, order), 0)
+    lane = lax.broadcasted_iota(jnp.int32, (PANEL, order), 1)
+    work = [gram[q * PANEL : (q + 1) * PANEL] for q in range(count)]
+    extra = [jnp.where(lane == row + q * PANEL, 1.0, 0.0) for q in range(count)]
+    upper = []
+    inverse = []
+    block = [column_of(work[0], k) for k in range(PANEL)]
+    for p in range(count):
+        base = p * PANEL
+        near = [q for q in range(p + 1, min(p + 1 + NEAR, count))]
+        beside = {q: [column_of(work[q], base + c) for c in range(PANEL)] for q in near}
+        following = [column_of(work[p + 1], base + PANEL + k) for k in range(PANEL)] if near else []
+        unit = [jnp.where(row == c, 1.0, 0.0) for c in range(PANEL)]
+        roots = jnp.zeros((PANEL, order), F32)
+        for r in range(PANEL):
+            root = lax.rsqrt(spread_rows(block[r], r, PANEL))
+            column = jnp.where(row > r, block[r] * root, 0.0)
+            rows = {k: spread_rows(column, k, PANEL) for k in range(r + 1, PANEL)}
+            for k in range(r + 1, PANEL):
+                block[k] = block[k] - column * rows[k]
+            for q in near:
+                beside[q][r] = beside[q][r] * root
+                for k in range(r + 1, PANEL):
+                    beside[q][k] = beside[q][k] - beside[q][r] * rows[k]
+            ratio = column * root
+            for c in range(r + 1):
+                unit[c] = unit[c] - ratio * spread_rows(unit[c], r, PANEL)
+            roots = jnp.where(row == r, root, roots)
+            if near:
+                done = beside[p + 1][r]
+                for k in range(PANEL):
+                    following[k] = following[k] - done * spread_rows(done, k, PANEL)
+        if p < len(fill):
+            fill[p]()
+        top = unit[0] * spread_rows(work[p], 0, PANEL)
+        side = unit[0] * spread_rows(extra[p], 0, PANEL)
+        for c in range(1, PANEL):
+            top = top + unit[c] * spread_rows(work[p], c, PANEL)
+            side = side + unit[c] * spread_rows(extra[p], c, PANEL)
+        top = jnp.where(lane >= row + base, top * roots, 0.0)
+        side = side * roots
+        upper.append(top)
+        inverse.append(side)
+        if near:
+            tops = [spread_rows(top, c, PANEL) for c in range(PANEL)]
+            sides = [spread_rows(side, c, PANEL) for c in range(PANEL)]
+            for q in near:
+                for c in range(PANEL):
+                    work[q] = work[q] - beside[q][c] * tops[c]
+                    extra[q] = extra[q] - beside[q][c] * sides[c]
+            if p + 1 + NEAR < count:
+                change = outer_change(top, side)
+                for q in range(p + 1 + NEAR, count):
+                    rows = slice(q * PANEL, (q + 1) * PANEL)
+                    work[q] = work[q] - change[rows, :order]
+                    extra[q] = extra[q] - change[rows, order:]
+            block = following
+    return jnp.concatenate(upper, axis=0), jnp.concatenate(inverse, axis=0)
+
+
+def lanczos_kernel(
+    place_ref,
+    x_own,
+    x_left1,
+    x_left2,
+    x_left3,
+    x_right1,
+    x_right2,
+    x_right3,
+    pairs_hbm,
+    alpha_ref,
+    beta_ref,
+    next_ref,
+    pairs,
+    xs,
+    ys,
+    qs,
+    flat,
+    sem,
+    rows_total,
+):
+    copy = pltpu.make_async_copy(pairs_hbm, pairs, sem)
+    copy.start()
+    place = place_ref[0]
+    core = place_ref[1]
+    orbitals, atoms, states = x_own.shape
+    half = atoms // 2
+    total = flat.shape[0]
+    scale = 1.0 / rows_total
+
+    def take(source, base):
+        xs[:, pl.ds(pl.multiple_of(base, half), source.shape[1]), :] = source[...]
+
+    take(x_own, place * atoms)
+    for step, (mine, other) in enumerate(
+        ((x_left1, x_right1), (x_left2, x_right2), (x_left3, x_right3)), 1
+    ):
+        base = (place ^ step) * atoms
+        take(mine, base + core * half)
+        take(other, base + (1 - core) * half)
+
+    def whole(ref):
+        return ref[...].reshape(total, states)
+
+    def own_gram(pieces):
+        high, low = pieces
+        both = dot(high, jnp.concatenate([high, low], axis=1), TN)
+        cross = both[:, states:]
+        return (both[:, :states] + (cross + jnp.transpose(cross))) * scale
+
+    def set_flat(pieces):
+        flat[:, :states] = pieces[0]
+        flat[:, states:] = pieces[1]
+
+    chunk = 208
+    width = 256
+
+    def forward(start):
+        def run():
+            both = dot(pairs[start : start + chunk, :], flat[...], NN)
+            ys[start : start + chunk, :] = both[:, :states] + both[:, states:]
+
+        return run
+
+    def backward(start):
+        stop = min(start + width, total)
+
+        def run():
+            both = dot(pairs[:, start:stop], flat[...], TN)
+            ys[start:stop, :] = ys[start:stop, :] + (both[:, :states] + both[:, states:])
+
+        return run
+
+    fill = [forward(start) for start in range(0, total, chunk)]
+    fill = fill + [backward(start) for start in range(0, total, width)]
+
+    pieces = split(whole(xs))
+    set_flat(pieces)
+    gram = own_gram(pieces)
+    copy.wait()
+    factor, inverse = factor_panels(gram, fill)
+    inverse = split(inverse)
+    current = dot_split(pieces, inverse, NT)
+    first = split(current)
+    qs[:, :states] = first[0]
+    qs[:, states:] = first[1]
+    residue = dot_split(split(ys[...]), inverse, NT)
+    alpha = dot_split(first, split(residue), TN) * scale
+    alpha_ref[0] = alpha
+    residue = residue - dot_split(first, split(alpha), NN)
+    pieces = split(residue)
+    set_flat(pieces)
+    gram = own_gram(pieces)
+    factor, inverse = factor_panels(gram, fill)
+    beta_ref[0] = factor
+    inverse = split(inverse)
+    current = dot_split((flat[:, :states], flat[:, states:]), inverse, NT)
+    residue = dot_split(split(ys[...]), inverse, NT)
+    residue = residue - dot_split((qs[:, :states], qs[:, states:]), split(factor), NT)
+    first = split(current)
+    alpha = dot_split(first, split(residue), TN) * scale
+    alpha_ref[1] = alpha
+    residue = residue - dot_split(first, split(alpha), NN)
+    xs[...] = residue.reshape(xs.shape)
+    gram = own_gram(split(residue))
+    factor, inverse = factor_panels(gram)
+    beta_ref[1] = factor
+    mine = xs[:, pl.ds(pl.multiple_of(place * atoms, atoms), atoms), :].reshape(orbitals * atoms, states)
+    mine = dot_split(split(mine), split(inverse), NT)
+    next_ref[...] = mine.reshape(orbitals, atoms, states)
+
+
+def run_lanczos(place, own, left, right, pairs, rows_total):
+    states = own.shape[2]
+    total = pairs.shape[0]
+    vmem = pl.BlockSpec(memory_space=pltpu.VMEM)
+
+    def kernel(*refs):
+        lanczos_kernel(*refs, rows_total)
+
+    return pl.pallas_call(
+        kernel,
+        out_shape=(
+            jax.ShapeDtypeStruct((STEPS, states, states), F32),
+            jax.ShapeDtypeStruct((STEPS, states, states), F32),
+            jax.ShapeDtypeStruct(own.shape, F32),
+        ),
+        in_specs=[pl.BlockSpec(memory_space=pltpu.SMEM)] + [vmem] * 7 + [pl.BlockSpec(memory_space=pl.ANY)],
+        out_specs=(vmem, vmem, vmem),
+        scratch_shapes=[
+            pltpu.VMEM(pairs.shape, BF16),
+            pltpu.VMEM((own.shape[0], total // own.shape[0], states), F32),
+            pltpu.VMEM((total, states), F32),
+            pltpu.VMEM((total, 2 * states), BF16),
+            pltpu.VMEM((total, 2 * states), BF16),
+            pltpu.SemaphoreType.DMA,
+        ],
+        compiler_params=pltpu.CompilerParams(vmem_limit_bytes=VMEM_LIMIT),
+        name="block_lanczos",
+    )(place, own, *left, *right, pairs)
+
+
+def exchange(shard, axis, mask):
+    devices = lax.axis_size(axis)
+    return lax.ppermute(shard, axis, [(i, i ^ mask) for i in range(devices)])
+
+
+def body(
+    node_feats,
+    distance,
+    neighbours,
+    counts,
+    w_source,
+    w_target,
+    w_radial,
+    w_middle,
+    w_output,
+    w_onsite,
+    initial,
+):
+    atoms_here, slots_here = neighbours.shape
+    domains = lax.axis_size("dom")
+    members = lax.axis_size("st") * lax.axis_size("sub")
+    atoms_all = atoms_here * domains
+    suits = (domains, atoms_all, 2 * members * slots_here, initial.shape[2]) == (4, LANES, LANES, LANES)
+    if not (suits and lax.axis_size("sub") == 2 and lax.axis_size("st") == 2):
+        return body_spread(
+            node_feats,
+            distance,
+            neighbours,
+            counts,
+            w_source,
+            w_target,
+            w_radial,
+            w_middle,
+            w_output,
+            w_onsite,
+            initial,
+        )
+    domain = lax.axis_index("dom")
+    core = lax.axis_index("sub")
+    member = lax.axis_index(("st", "sub"))
+    place = jnp.stack([domain, core, member]).astype(jnp.int32)
+
+    own = run_lanes(place, distance.T, neighbours.T, counts.reshape(1, atoms_here))
+    own = own + exchange(own, "sub", 1)
+    own = own + exchange(own, "st", 1)
+    wide = node_feats.astype(F32)
+    pack = jnp.concatenate([own.reshape(atoms_here, LANES), wide[:, :LANES], wide[:, LANES:]], axis=0)
+    packs = [exchange(pack, "dom", step) for step in range(1, domains)]
+
+    states = jnp.swapaxes(initial, 0, 1)
+    half = atoms_here // 2
+    part = lax.dynamic_slice_in_dim(states, core * half, half, 1)
+    part, packs = lax.optimization_barrier((part, packs))
+    left = [exchange(part, "dom", step) for step in range(1, domains)]
+
+    weights = (w_source, w_target, w_radial, w_middle, w_output.T, w_onsite.T)
+    pairs = run_network(place, [pack] + packs, weights)
+    left, pairs = lax.optimization_barrier((left, pairs))
+    right = [exchange(piece, "sub", 1) for piece in left]
+    pairs = pairs.reshape(ORB * atoms_all, ORB * LANES)
+    alpha_blocks, beta_blocks, last = run_lanczos(place, states, left, right, pairs, float(atoms_all * ORB))
+    return (alpha_blocks, beta_blocks, jnp.swapaxes(last, 0, 1))
+
+
 def solution(mesh):
     placed = (
         P(("grp", "dom"), None),

time: 1620 us -> 65.8 us (0.04); the launches traced: 1600 us -> 65.4 us
  local copies, waits for them, and re-layouts: 510 us -> 2.28 us
  matrix products: 428 us -> 0 us
  loops' own time: 293 us -> 0 us
  waiting for transfers between devices: 218 us -> 6.73 us
  other arithmetic: 129 us -> 1.34 us
  Pallas kernels: 0 us -> 40.9 us
    dynamic_slice x768 -> x1, local copies, waits for them, and re-layouts: 452 us -> 0.9 us  [body(): part = lax.dynamic_slice_in_dim(states, core * half, half, 1)]
    dot_general x406 -> x0, matrix products: 428 us -> none  [the longest x384 393 us: row_step(): known = jnp.dot(factor_row, inverse, precision=lax.Precision.HIGHEST)]
    another operation x6 -> x0, loops' own time: 293 us -> none  [the longest x3 282 us: upper_factor(): lax.fori_loop(0, order, column_step, (matrix, jnp.zeros_like(matrix)))]
    psum x7 -> x0, waiting for transfers between devices: 218 us -> none  [the longest x5 154 us: totals(): return lax.psum(value, 'dom')]
    scatter-add x2 -> x0, other arithmetic: 80.4 us -> none  [edge_terms(): jax.ops.segment_sum(backward.reshape(-1, ORB, whole_rows.shape[-1]), loca...]
    pallas_call x0 -> x3, Pallas kernels: none -> 40.9 us  [the longest x1 22.5 us: run_lanczos(): pl.pallas_call(kernel, out_shape=(jax.ShapeDtypeStruct((STEPS, states, st...]
    sub x385 -> x0, other arithmetic: 32.6 us -> none  [the longest x384 31.5 us: column_step(): work = work - scaled[:, None] * scaled[None, :]]
    dynamic_update_slice x768 -> x0, local copies, waits for them, and re-layouts: 26.1 us -> none  [the longest x384 14.3 us: column_step(): lax.dynamic_update_slice_in_dim(lower, scaled[:, None], column_index, 1)]
  transfers between devices with their start and end apart: 12 -> 11, of which waited for: 7 -> 7; matrix products, arithmetic and copies ran while one was open for 8% -> 2% of each run, Pallas kernels for 0% -> 26%
where the time goes in v2:
time: 65.8 us; the launch traced here: 65.4 us
  Pallas kernels  40.9 us (62%)
  starting transfers between devices  13.2 us (20%)
  waiting for transfers between devices  6.73 us (10%)
  local copies, waits for them, and re-layouts  2.28 us (3%)
  other arithmetic  1.34 us (2%)
  between operations  0.9 us (1%)
    pallas_call x1, Pallas kernels, run_lanczos(): pl.pallas_call(kernel, out_shape=(jax.ShapeDtypeStruct((STEPS, states, st...  22.5 us
    pallas_call x1, Pallas kernels, run_network(): pl.pallas_call(network_kernel, grid=(domains, groups), out_shape=jax.Shap...  16.9 us
    ppermute x11, starting transfers between devices, exchange(): return lax.ppermute(shard, axis, [(i, i ^ mask) for i in range(devices)])  13.2 us
    ppermute x11, waiting for transfers between devices, exchange(): return lax.ppermute(shard, axis, [(i, i ^ mask) for i in range(devices)])  6.73 us
    pallas_call x1, Pallas kernels, run_lanes(): pl.pallas_call(lanes_kernel, out_shape=jax.ShapeDtypeStruct((2, distance....  1.62 us
  transfers between devices with their start and end apart: 11, of which 7 were waited for; matrix products, arithmetic and copies ran while one was open for 2% of the time, Pallas kernels for 26%

profile of v2, /device:TPU:0, one launch (start us, length us, event | category | flops | bytes accessed | tf_op | source)
XLA Modules:
  0.0 65.4 jit_solution(9104540328502353326)
XLA Ops:
  0.6 0.6 pad_add_fusion.place_ref.refs_0_
  1.2 1.6 %slot_lanes.1 = f32[2,16,128]{2,1,0:T(8,128)} custom-call(s32[3]{0:T(128)} %pad_add_fusion.place_ref.refs_0_, f32[16,32]{1,0:T(8,128)} %bitcast.17, s32[16,32]{1,0:T(8,128)} %bitcast.18, s32[1,32]{1,0:T(1,128)} %bitcast.19), custom_call_target="tpu_custom_call" | custom-call | tf_op jit(solution)/shard_map/slot_lanes/pallas_call | solution.py:245
  2.9 0.5 collective-permute-start
  3.3 1.0 %collective-permute-done = f32[2,16,128]{2,1,0:T(8,128)S(1)} collective-permute-done((f32[2,16,128]{2,1,0:T(8,128)}, f32[2,16,128]{2,1,0:T(8,128)S(1)}, u32[]{:S(2)}, u32[]{:S(2)}) %collective-permute-start) | collective-permute-done | bytes 16416 | tf_op jit(solution)/shard_map/ppermute | solution.py:652
  4.4 0.7 %add.14 = f32[2,16,128]{2,1,0:T(8,128)S(1)} add(f32[2,16,128]{2,1,0:T(8,128)} %slot_lanes.1, f32[2,16,128]{2,1,0:T(8,128)S(1)} %collective-permute-done) | non-fusion elementwise | flops 4096 | bytes 49152 | tf_op jit(solution)/shard_map/add | solution.py:693
  5.1 2.8 %collective-permute-start.1 = (f32[2,16,128]{2,1,0:T(8,128)S(1)}, f32[2,16,128]{2,1,0:T(8,128)S(1)}, u32[]{:S(2)}, u32[]{:S(2)}) collective-permute-start(f32[2,16,128]{2,1,0:T(8,128)S(1)} %add.14), channel_id=1, source_target_pairs={{0,2},{2,0},{1,3},{3,1},{4,6},{6,4},{5,7},{7,5},{8,10},{10,8},{9,1... | collective-permute-start | bytes 49160 | tf_op jit(solution)/shard_map/ppermute | solution.py:652
  7.9 0.7 %fusion = (f32[32,128]{1,0:T(8,128)S(1)}, f32[32,128]{1,0:T(8,128)S(1)}) fusion(bf16[32,256]{1,0:T(8,128)(2,1)} %param.11), kind=kLoop, calls=%fused_computation.3 | loop fusion | bytes 65536 | tf_op jit(solution)/shard_map/slice | solution.py:696
  8.6 1.0 %collective-permute-done.1 = f32[2,16,128]{2,1,0:T(8,128)S(1)} collective-permute-done((f32[2,16,128]{2,1,0:T(8,128)S(1)}, f32[2,16,128]{2,1,0:T(8,128)S(1)}, u32[]{:S(2)}, u32[]{:S(2)}) %collective-permute-start.1) | collective-permute-done | bytes 16416 | tf_op jit(solution)/shard_map/ppermute | solution.py:652
  9.7 0.0 copy-start.6
  9.7 4.2 %collective-permute-start.4 = (f32[96,128]{1,0:T(8,128)S(1)}, f32[96,128]{1,0:T(8,128)S(1)}, u32[]{:S(2)}, u32[]{:S(2)}) collective-permute-start(f32[96,128]{1,0:T(8,128)S(1)} %pad_maximum_fusion.pack0), channel_id=1, source_target_pairs={{0,12},{4,8},{8,4},{12,0},{1,13},{5,9},{9,5},{13,1},{2,14},{6,10},... | collective-permute-start | bytes 147464 | tf_op jit(solution)/shard_map/ppermute | solution.py:652
  13.9 0.0 collective-permute-start.3
  13.9 0.6 collective-permute-start.2
  14.5 0.9 %dynamic-slice_bitcast_fusion = f32[13,16,128]{2,1,0:T(8,128)S(1)} fusion(f32[32,13,128]{2,0,1:T(8,128)} %param.21, s32[]{:T(128)S(6)} %select_n.3), kind=kLoop, calls=%fused_computation | loop fusion | bytes 212996 | tf_op jit(solution)/shard_map/dynamic_slice | solution.py:701
  15.4 0.8 %collective-permute-done.4.pack3 = f32[96,128]{1,0:T(8,128)S(1)} collective-permute-done((f32[96,128]{1,0:T(8,128)S(1)}, f32[96,128]{1,0:T(8,128)S(1)}, u32[]{:S(2)}, u32[]{:S(2)}) %collective-permute-start.4) | collective-permute-done | bytes 49184 | tf_op jit(solution)/shard_map/ppermute | solution.py:652
  16.2 0.0 copy-start.7
  16.3 2.6 %collective-permute-done.3.pack2 = f32[96,128]{1,0:T(8,128)S(1)} collective-permute-done((f32[96,128]{1,0:T(8,128)S(1)}, f32[96,128]{1,0:T(8,128)S(1)}, u32[]{:S(2)}, u32[]{:S(2)}) %collective-permute-start.3) | collective-permute-done | bytes 49184 | tf_op jit(solution)/shard_map/ppermute | solution.py:652
  18.9 0.0 copy-start.8
  18.9 0.0 collective-permute-done.2.pack1
  18.9 0.0 copy-start.9
  18.9 1.6 %collective-permute-start.7 = (f32[13,16,128]{2,1,0:T(8,128)S(1)}, f32[13,16,128]{2,1,0:T(8,128)S(1)}, u32[]{:S(2)}, u32[]{:S(2)}) collective-permute-start(f32[13,16,128]{2,1,0:T(8,128)S(1)} %dynamic-slice_bitcast_fusion), channel_id=1, source_target_pairs={{0,12},{4,8},{8,4},{12,0},{1,13},{5,9},{9,5},{13,1},{2,14},{6,10},... | collective-permute-start | bytes 319496 | tf_op jit(solution)/shard_map/ppermute | solution.py:652
  20.5 0.4 collective-permute-start.6
  20.9 2.4 %collective-permute-start.5 = (f32[13,16,128]{2,1,0:T(8,128)S(1)}, f32[13,16,128]{2,1,0:T(8,128)S(1)}, u32[]{:S(2)}, u32[]{:S(2)}) collective-permute-start(f32[13,16,128]{2,1,0:T(8,128)S(1)} %dynamic-slice_bitcast_fusion), channel_id=1, source_target_pairs={{0,4},{4,0},{8,12},{12,8},{1,5},{5,1},{9,13},{13,9},{2,6},{6,2},{1... | collective-permute-start | bytes 319496 | tf_op jit(solution)/shard_map/ppermute | solution.py:652
  23.3 0.0 copy-done.6
  23.3 0.0 copy-done.7
  23.3 0.0 copy-done.8
  23.3 0.0 copy-done.9
  23.3 16.9 %pair_network.1 = bf16[13,128,1664]{2,1,0:T(8,128)(2,1)} custom-call(s32[3]{0:T(128)} %pad_add_fusion.place_ref.refs_0_, f32[96,128]{1,0:T(8,128)} %copy-done.6, f32[96,128]{1,0:T(8,128)} %copy-done.9, f32[96,128]{1,0:T(8,128)} %copy-done.8, f32[96,128]{1,0:T(8,128)} %copy-done.7, bf16[256,256]{1,0:T(8,128)(2,1)} %w_source.1, bf16[256,256]{1,0:T(8,128)(2,1)} %w_target.1, ...), custom_call_target="tpu_custom_call" | custom-call | flops 6000000000 | bytes 8000000 | tf_op jit(solution)/shard_map/pair_network/pallas_call | solution.py:399
  40.2 0.0 collective-permute-done.7.refs_4_
  40.2 0.0 copy-start
  40.2 0.0 collective-permute-done.6.refs_3_
  40.2 0.0 copy-start.1
  40.2 0.0 collective-permute-done.5.refs_2_
  40.2 0.0 copy-start.2
  40.2 0.1 collective-permute-start.8
  40.3 0.5 collective-permute-start.9
  40.8 0.1 collective-permute-start.10
  40.9 0.7 %collective-permute-done.8.refs_5_ = f32[13,16,128]{2,1,0:T(8,128)S(1)} collective-permute-done((f32[13,16,128]{2,1,0:T(8,128)S(1)}, f32[13,16,128]{2,1,0:T(8,128)S(1)}, u32[]{:S(2)}, u32[]{:S(2)}) %collective-permute-start.8) | collective-permute-done | bytes 106528 | tf_op jit(solution)/shard_map/ppermute | solution.py:652
  41.6 0.0 copy-start.3
  41.6 0.1 collective-permute-done.9.refs_6_
  41.8 0.0 copy-start.4
  41.8 0.4 collective-permute-done.10.refs_7_
  42.1 0.0 copy-done
  42.1 0.0 copy-done.1
  42.1 0.0 copy-done.2
  42.1 0.1 copy-done.3
  42.2 0.2 copy-done.4
  42.4 0.4 copy-done.5
  42.8 22.5 %block_lanczos.1 = (f32[2,128,128]{2,1,0:T(8,128)}, f32[2,128,128]{2,1,0:T(8,128)}, f32[13,32,128]{2,1,0:T(8,128)}) custom-call(s32[3]{0:T(128)} %pad_add_fusion.place_ref.refs_0_, f32[13,32,128]{2,1,0:T(8,128)} %bitcast.15, f32[13,16,128]{2,1,0:T(8,128)} %copy-done.2, f32[13,16,128]{2,1,0:T(8,128)} %copy-done.1, f32[13,16,128]{2,1,0:T(8,128)} %copy-done, ...), custom_call_target="tpu_custom_call" | custom-call | tf_op jit(solution)/shard_map/block_lanczos/pallas_call | solution.py:628
  (3 shorter events, 0.0 us)
Async XLA Ops:
  2.9 1.5 %collective-permute-start = (f32[2,16,128]{2,1,0:T(8,128)}, f32[2,16,128]{2,1,0:T(8,128)S(1)}, u32[]{:S(2)}, u32[]{:S(2)}) collective-permute-start(f32[2,16,128]{2,1,0:T(8,128)} %slot_lanes.1), channel_id=1, source_target_pairs={{0,1},{1,0},{2,3},{3,2},{4,5},{5,4},{6,7},{7,6},{8,9},{9,8},{10,11... | collective-permute-start | bytes 49160 | tf_op jit(solution)/shard_map/ppermute | solution.py:652
  5.1 4.5 %collective-permute-start.1 = (f32[2,16,128]{2,1,0:T(8,128)S(1)}, f32[2,16,128]{2,1,0:T(8,128)S(1)}, u32[]{:S(2)}, u32[]{:S(2)}) collective-permute-start(f32[2,16,128]{2,1,0:T(8,128)S(1)} %add.14), channel_id=1, source_target_pairs={{0,2},{2,0},{1,3},{3,1},{4,6},{6,4},{5,7},{7,5},{8,10},{10,8},{9,1... | collective-permute-start | bytes 49160 | tf_op jit(solution)/shard_map/ppermute | solution.py:652
  9.7 13.7 %copy-start.6 = (f32[96,128]{1,0:T(8,128)}, f32[96,128]{1,0:T(8,128)S(1)}, u32[]{:S(2)}) copy-start(f32[96,128]{1,0:T(8,128)S(1)} %pad_maximum_fusion.pack0) | copy-start | bytes 147460
  9.7 6.6 %collective-permute-start.4 = (f32[96,128]{1,0:T(8,128)S(1)}, f32[96,128]{1,0:T(8,128)S(1)}, u32[]{:S(2)}, u32[]{:S(2)}) collective-permute-start(f32[96,128]{1,0:T(8,128)S(1)} %pad_maximum_fusion.pack0), channel_id=1, source_target_pairs={{0,12},{4,8},{8,4},{12,0},{1,13},{5,9},{9,5},{13,1},{2,14},{6,10},... | collective-permute-start | bytes 147464 | tf_op jit(solution)/shard_map/ppermute | solution.py:652
  13.9 5.0 %collective-permute-start.3 = (f32[96,128]{1,0:T(8,128)S(1)}, f32[96,128]{1,0:T(8,128)S(1)}, u32[]{:S(2)}, u32[]{:S(2)}) collective-permute-start(f32[96,128]{1,0:T(8,128)S(1)} %pad_maximum_fusion.pack0), channel_id=1, source_target_pairs={{0,8},{4,12},{8,0},{12,4},{1,9},{5,13},{9,1},{13,5},{2,10},{6,14},... | collective-permute-start | bytes 147464 | tf_op jit(solution)/shard_map/ppermute | solution.py:652
  13.9 5.0 %collective-permute-start.2 = (f32[96,128]{1,0:T(8,128)S(1)}, f32[96,128]{1,0:T(8,128)S(1)}, u32[]{:S(2)}, u32[]{:S(2)}) collective-permute-start(f32[96,128]{1,0:T(8,128)S(1)} %pad_maximum_fusion.pack0), channel_id=1, source_target_pairs={{0,4},{4,0},{8,12},{12,8},{1,5},{5,1},{9,13},{13,9},{2,6},{6,2},{1... | collective-permute-start | bytes 147464 | tf_op jit(solution)/shard_map/ppermute | solution.py:652
  16.2 7.1 %copy-start.7 = (f32[96,128]{1,0:T(8,128)}, f32[96,128]{1,0:T(8,128)S(1)}, u32[]{:S(2)}) copy-start(f32[96,128]{1,0:T(8,128)S(1)} %collective-permute-done.4.pack3) | copy-start | bytes 147460
  18.9 4.5 %copy-start.8 = (f32[96,128]{1,0:T(8,128)}, f32[96,128]{1,0:T(8,128)S(1)}, u32[]{:S(2)}) copy-start(f32[96,128]{1,0:T(8,128)S(1)} %collective-permute-done.3.pack2) | copy-start | bytes 147460
  18.9 4.5 %copy-start.9 = (f32[96,128]{1,0:T(8,128)}, f32[96,128]{1,0:T(8,128)S(1)}, u32[]{:S(2)}) copy-start(f32[96,128]{1,0:T(8,128)S(1)} %collective-permute-done.2.pack1) | copy-start | bytes 147460
  18.9 21.3 %collective-permute-start.7 = (f32[13,16,128]{2,1,0:T(8,128)S(1)}, f32[13,16,128]{2,1,0:T(8,128)S(1)}, u32[]{:S(2)}, u32[]{:S(2)}) collective-permute-start(f32[13,16,128]{2,1,0:T(8,128)S(1)} %dynamic-slice_bitcast_fusion), channel_id=1, source_target_pairs={{0,12},{4,8},{8,4},{12,0},{1,13},{5,9},{9,5},{13,1},{2,14},{6,10},... | collective-permute-start | bytes 319496 | tf_op jit(solution)/shard_map/ppermute | solution.py:652
  20.5 19.7 %collective-permute-start.6 = (f32[13,16,128]{2,1,0:T(8,128)S(1)}, f32[13,16,128]{2,1,0:T(8,128)S(1)}, u32[]{:S(2)}, u32[]{:S(2)}) collective-permute-start(f32[13,16,128]{2,1,0:T(8,128)S(1)} %dynamic-slice_bitcast_fusion), channel_id=1, source_target_pairs={{0,8},{4,12},{8,0},{12,4},{1,9},{5,13},{9,1},{13,5},{2,10},{6,14},... | collective-permute-start | bytes 319496 | tf_op jit(solution)/shard_map/ppermute | solution.py:652
  20.9 19.3 %collective-permute-start.5 = (f32[13,16,128]{2,1,0:T(8,128)S(1)}, f32[13,16,128]{2,1,0:T(8,128)S(1)}, u32[]{:S(2)}, u32[]{:S(2)}) collective-permute-start(f32[13,16,128]{2,1,0:T(8,128)S(1)} %dynamic-slice_bitcast_fusion), channel_id=1, source_target_pairs={{0,4},{4,0},{8,12},{12,8},{1,5},{5,1},{9,13},{13,9},{2,6},{6,2},{1... | collective-permute-start | bytes 319496 | tf_op jit(solution)/shard_map/ppermute | solution.py:652
  40.2 1.9 %copy-start = (f32[13,16,128]{2,1,0:T(8,128)}, f32[13,16,128]{2,1,0:T(8,128)S(1)}, u32[]{:S(2)}) copy-start(f32[13,16,128]{2,1,0:T(8,128)S(1)} %collective-permute-done.7.refs_4_) | copy-start | bytes 319492
  40.2 1.9 %copy-start.1 = (f32[13,16,128]{2,1,0:T(8,128)}, f32[13,16,128]{2,1,0:T(8,128)S(1)}, u32[]{:S(2)}) copy-start(f32[13,16,128]{2,1,0:T(8,128)S(1)} %collective-permute-done.6.refs_3_) | copy-start | bytes 319492
  40.2 1.9 %copy-start.2 = (f32[13,16,128]{2,1,0:T(8,128)}, f32[13,16,128]{2,1,0:T(8,128)S(1)}, u32[]{:S(2)}) copy-start(f32[13,16,128]{2,1,0:T(8,128)S(1)} %collective-permute-done.5.refs_2_) | copy-start | bytes 319492
  40.2 1.4 %collective-permute-start.8 = (f32[13,16,128]{2,1,0:T(8,128)S(1)}, f32[13,16,128]{2,1,0:T(8,128)S(1)}, u32[]{:S(2)}, u32[]{:S(2)}) collective-permute-start(f32[13,16,128]{2,1,0:T(8,128)S(1)} %collective-permute-done.5.refs_2_), channel_id=1, source_target_pairs={{0,1},{1,0},{2,3},{3,2},{4,5},{5,4},{6,7},{7,6},{8,9},{9,8},{10,11... | collective-permute-start | bytes 319496 | tf_op jit(solution)/shard_map/ppermute | solution.py:652
  40.3 1.5 %collective-permute-start.9 = (f32[13,16,128]{2,1,0:T(8,128)S(1)}, f32[13,16,128]{2,1,0:T(8,128)S(1)}, u32[]{:S(2)}, u32[]{:S(2)}) collective-permute-start(f32[13,16,128]{2,1,0:T(8,128)S(1)} %collective-permute-done.6.refs_3_), channel_id=1, source_target_pairs={{0,1},{1,0},{2,3},{3,2},{4,5},{5,4},{6,7},{7,6},{8,9},{9,8},{10,11... | collective-permute-start | bytes 319496 | tf_op jit(solution)/shard_map/ppermute | solution.py:652
  40.8 1.3 %collective-permute-start.10 = (f32[13,16,128]{2,1,0:T(8,128)S(1)}, f32[13,16,128]{2,1,0:T(8,128)S(1)}, u32[]{:S(2)}, u32[]{:S(2)}) collective-permute-start(f32[13,16,128]{2,1,0:T(8,128)S(1)} %collective-permute-done.7.refs_4_), channel_id=1, source_target_pairs={{0,1},{1,0},{2,3},{3,2},{4,5},{5,4},{6,7},{7,6},{8,9},{9,8},{10,11... | collective-permute-start | bytes 319496 | tf_op jit(solution)/shard_map/ppermute | solution.py:652
  41.6 0.6 copy-start.3
  41.8 0.6 copy-start.4
  42.1 0.6 copy-start.5

commit v3 on v2

--- a/solution.py
+++ b/solution.py
@@ -186,6 +186,7 @@
 LANES = 128
 PAD = 16
 PANEL = 8
+SKEW = 8
 NEAR = 3
 VMEM_LIMIT = 56 * 1024 * 1024
 
@@ -223,9 +224,9 @@
     return jnp.broadcast_to(value[row : row + 1, :], (count, value.shape[1]))
 
 
-def lanes_kernel(place_ref, distance, named, counts, out_ref):
+def lanes_kernel(distance, named, counts, out_ref):
     slots, atoms = distance.shape
-    member = place_ref[2]
+    member = lax.axis_index(("st", "sub"))
     slot = lax.broadcasted_iota(jnp.int32, (slots, atoms), 0) + member * slots
     usable = slot < counts[...]
     names = jnp.where(usable, named[...], -1).astype(F32)
@@ -240,19 +241,18 @@
         out_ref[kind] = pltpu.roll(row, member * slots, 1)
 
 
-def run_lanes(place, distance, named, counts):
+def run_lanes(distance, named, counts):
     vmem = pl.BlockSpec(memory_space=pltpu.VMEM)
     return pl.pallas_call(
         lanes_kernel,
         out_shape=jax.ShapeDtypeStruct((2, distance.shape[1] // 2, LANES), F32),
-        in_specs=[pl.BlockSpec(memory_space=pltpu.SMEM), vmem, vmem, vmem],
+        in_specs=[vmem, vmem, vmem],
         out_specs=vmem,
         name="slot_lanes",
-    )(place, distance, named, counts)
+    )(distance, named, counts)
 
 
 def network_kernel(
-    place_ref,
     pack0,
     pack1,
     pack2,
@@ -284,11 +284,11 @@
     atoms = source.shape[1]
     tiles = atoms // 4
     basis = w_radial.shape[0]
-    stride = ORB * PAD
+    stride = ORB * PAD + SKEW
 
     @pl.when((domain == 0) & (group == 0))
     def prepare():
-        place = place_ref[0]
+        place = lax.axis_index("dom")
         for step, pack in enumerate((pack0, pack1, pack2, pack3)):
             where = place ^ step
             reach = pack[: 2 * tiles]
@@ -300,7 +300,6 @@
             source[where] = dot(got, w_source[...], NN)
             target[where] = dot(got, w_target[...], NN)
             feats[where] = got
-        middle[...] = jnp.transpose(w_middle[...].astype(F32)).astype(BF16)
         empty = jnp.zeros((PAD - ORB, rows.shape[1]), F32)
 
         def fill_raw(weights):
@@ -338,7 +337,7 @@
             ],
             axis=0,
         )
-        mixer[...] = jnp.transpose(stacked).astype(BF16)
+        mixer[...] = stacked.astype(BF16)
 
     lane = lax.broadcasted_iota(jnp.int32, (1, LANES), 1)
     upper = lane >= LANES // 2
@@ -366,9 +365,9 @@
             ).astype(BF16)
         )
     columns = jnp.concatenate(inputs, axis=1)
-    hidden = silu(dot(mixer[...], columns, NN)).astype(BF16)
-    second = silu(dot(middle[...], hidden, NN)).astype(BF16)
-    blocks = dot(outer[...], second, NN)
+    hidden = silu(dot(columns, mixer[...], TN)).astype(BF16)
+    second = silu(dot(hidden, w_middle[...], NN)).astype(BF16)
+    blocks = dot(outer[...], second, NT)
     flags = jnp.concatenate(
         [jnp.where(column2 < LANES // 2, row2, -2), jnp.where(column2 < LANES // 2, -2, row2)], axis=0
     )
@@ -380,7 +379,7 @@
             place = h * tiles + u
             atom = domain * atoms + group * 2 * tiles + place
             whole = placed[:, h * LANES : (h + 1) * LANES] + jnp.where(lane == atom, onsite[...], 0.0)
-            rows_at = slice(place * stride, (place + 1) * stride)
+            rows_at = slice(place * stride, place * stride + ORB * PAD)
             placed_ref[rows_at, :] = whole
     for j in range(ORB):
         for i in range(ORB):
@@ -388,7 +387,7 @@
             out_ref[i, :, j * LANES : (j + 1) * LANES] = tile.astype(BF16)
 
 
-def run_network(place, packs, weights):
+def run_network(packs, weights):
     domains = len(packs)
     atoms = packs[0].shape[0] // 3
     groups = 2
@@ -400,7 +399,7 @@
         network_kernel,
         grid=(domains, groups),
         out_shape=jax.ShapeDtypeStruct((ORB, domains * atoms, width), BF16),
-        in_specs=[pl.BlockSpec(memory_space=pltpu.SMEM)] + [vmem] * (domains + len(weights)),
+        in_specs=[vmem] * (domains + len(weights)),
         out_specs=pl.BlockSpec((ORB, 2 * tiles, width), lambda d, g: (0, groups * d + g, 0)),
         scratch_shapes=[
             pltpu.VMEM((domains, 2, 2 * tiles, LANES), F32),
@@ -414,12 +413,12 @@
             pltpu.VMEM((ORB * PAD, hidden), BF16),
             pltpu.VMEM((hidden // LANES, ORB * ORB, LANES), F32),
             pltpu.VMEM((ORB * PAD, hidden), F32),
-            pltpu.VMEM((2 * tiles * ORB * PAD, LANES), F32),
+            pltpu.VMEM((2 * tiles * (ORB * PAD + SKEW), LANES), F32),
         ],
         compiler_params=pltpu.CompilerParams(vmem_limit_bytes=VMEM_LIMIT),
         cost_estimate=pl.CostEstimate(flops=6_000_000_000, bytes_accessed=8_000_000, transcendentals=6_000_000),
         name="pair_network",
-    )(place, *packs, *weights)
+    )(*packs, *weights)
 
 
 def column_of(value, lane):
@@ -506,7 +505,6 @@
 
 
 def lanczos_kernel(
-    place_ref,
     x_own,
     x_left1,
     x_left2,
@@ -528,8 +526,8 @@
 ):
     copy = pltpu.make_async_copy(pairs_hbm, pairs, sem)
     copy.start()
-    place = place_ref[0]
-    core = place_ref[1]
+    place = lax.axis_index("dom")
+    core = lax.axis_index("sub")
     orbitals, atoms, states = x_own.shape
     half = atoms // 2
     total = flat.shape[0]
@@ -581,43 +579,57 @@
     fill = [forward(start) for start in range(0, total, chunk)]
     fill = fill + [backward(start) for start in range(0, total, width)]
 
+    def side(pieces):
+        return jnp.concatenate(pieces, axis=1)
+
+    def fold(both):
+        return both[:, :states] + both[:, states:]
+
+    def times(left, right):
+        return fold(dot(left, jnp.concatenate([side(right), side(right)], axis=0), NN))
+
+    def times_turned(left, right):
+        high, low = right
+        wide = jnp.concatenate([side((high, high)), side((low, low))], axis=0)
+        return fold(dot(left, wide, NT))
+
+    def overlap(left, right):
+        both = fold(dot(left, right, TN))
+        return (both[:states] + both[states:]) * scale
+
     pieces = split(whole(xs))
     set_flat(pieces)
     gram = own_gram(pieces)
     copy.wait()
     factor, inverse = factor_panels(gram, fill)
     inverse = split(inverse)
-    current = dot_split(pieces, inverse, NT)
-    first = split(current)
-    qs[:, :states] = first[0]
-    qs[:, states:] = first[1]
-    residue = dot_split(split(ys[...]), inverse, NT)
-    alpha = dot_split(first, split(residue), TN) * scale
+    first = side(split(times_turned(flat[...], inverse)))
+    qs[...] = first
+    residue = times_turned(side(split(ys[...])), inverse)
+    alpha = overlap(first, side(split(residue)))
     alpha_ref[0] = alpha
-    residue = residue - dot_split(first, split(alpha), NN)
+    residue = residue - times(first, split(alpha))
     pieces = split(residue)
     set_flat(pieces)
     gram = own_gram(pieces)
     factor, inverse = factor_panels(gram, fill)
     beta_ref[0] = factor
     inverse = split(inverse)
-    current = dot_split((flat[:, :states], flat[:, states:]), inverse, NT)
-    residue = dot_split(split(ys[...]), inverse, NT)
-    residue = residue - dot_split((qs[:, :states], qs[:, states:]), split(factor), NT)
-    first = split(current)
-    alpha = dot_split(first, split(residue), TN) * scale
+    first = side(split(times_turned(flat[...], inverse)))
+    residue = times_turned(side(split(ys[...])), inverse) - times_turned(qs[...], split(factor))
+    alpha = overlap(first, side(split(residue)))
     alpha_ref[1] = alpha
-    residue = residue - dot_split(first, split(alpha), NN)
+    residue = residue - times(first, split(alpha))
     xs[...] = residue.reshape(xs.shape)
     gram = own_gram(split(residue))
     factor, inverse = factor_panels(gram)
     beta_ref[1] = factor
     mine = xs[:, pl.ds(pl.multiple_of(place * atoms, atoms), atoms), :].reshape(orbitals * atoms, states)
-    mine = dot_split(split(mine), split(inverse), NT)
+    mine = times_turned(side(split(mine)), split(inverse))
     next_ref[...] = mine.reshape(orbitals, atoms, states)
 
 
-def run_lanczos(place, own, left, right, pairs, rows_total):
+def run_lanczos(own, left, right, pairs, rows_total):
     states = own.shape[2]
     total = pairs.shape[0]
     vmem = pl.BlockSpec(memory_space=pltpu.VMEM)
@@ -632,7 +644,7 @@
             jax.ShapeDtypeStruct((STEPS, states, states), F32),
             jax.ShapeDtypeStruct(own.shape, F32),
         ),
-        in_specs=[pl.BlockSpec(memory_space=pltpu.SMEM)] + [vmem] * 7 + [pl.BlockSpec(memory_space=pl.ANY)],
+        in_specs=[vmem] * 7 + [pl.BlockSpec(memory_space=pl.ANY)],
         out_specs=(vmem, vmem, vmem),
         scratch_shapes=[
             pltpu.VMEM(pairs.shape, BF16),
@@ -644,7 +656,7 @@
         ],
         compiler_params=pltpu.CompilerParams(vmem_limit_bytes=VMEM_LIMIT),
         name="block_lanczos",
-    )(place, own, *left, *right, pairs)
+    )(own, *left, *right, pairs)
 
 
 def exchange(shard, axis, mask):
@@ -687,27 +699,26 @@
     domain = lax.axis_index("dom")
     core = lax.axis_index("sub")
     member = lax.axis_index(("st", "sub"))
-    place = jnp.stack([domain, core, member]).astype(jnp.int32)
-
-    own = run_lanes(place, distance.T, neighbours.T, counts.reshape(1, atoms_here))
+
+    own = run_lanes(distance.T, neighbours.T, counts.reshape(1, atoms_here))
+    states = jnp.swapaxes(initial, 0, 1)
+    half = atoms_here // 2
+    part = lax.dynamic_slice_in_dim(states, core * half, half, 1)
+    left = [exchange(part, "dom", step) for step in range(1, domains)]
     own = own + exchange(own, "sub", 1)
     own = own + exchange(own, "st", 1)
     wide = node_feats.astype(F32)
     pack = jnp.concatenate([own.reshape(atoms_here, LANES), wide[:, :LANES], wide[:, LANES:]], axis=0)
-    packs = [exchange(pack, "dom", step) for step in range(1, domains)]
-
-    states = jnp.swapaxes(initial, 0, 1)
-    half = atoms_here // 2
-    part = lax.dynamic_slice_in_dim(states, core * half, half, 1)
-    part, packs = lax.optimization_barrier((part, packs))
-    left = [exchange(part, "dom", step) for step in range(1, domains)]
+    packs = [exchange(pack, "dom", 1), exchange(pack, "dom", 2)]
+    packs = packs + [exchange(packs[0], "dom", 2)]
+
 
     weights = (w_source, w_target, w_radial, w_middle, w_output.T, w_onsite.T)
-    pairs = run_network(place, [pack] + packs, weights)
-    left, pairs = lax.optimization_barrier((left, pairs))
+    packs, left = lax.optimization_barrier((packs, left))
     right = [exchange(piece, "sub", 1) for piece in left]
+    pairs = run_network([pack] + packs, weights)
     pairs = pairs.reshape(ORB * atoms_all, ORB * LANES)
-    alpha_blocks, beta_blocks, last = run_lanczos(place, states, left, right, pairs, float(atoms_all * ORB))
+    alpha_blocks, beta_blocks, last = run_lanczos(states, left, right, pairs, float(atoms_all * ORB))
     return (alpha_blocks, beta_blocks, jnp.swapaxes(last, 0, 1))
 
 

time: 65.8 us -> 60.6 us (0.921)
  Pallas kernels: 40.9 us -> 36.9 us
  waiting for transfers between devices: 6.73 us -> 5.41 us
  starting transfers between devices: 13.2 us -> 13.9 us
    pallas_call x1, Pallas kernels: 16.9 us -> 13.6 us  [run_network(): pl.pallas_call(network_kernel, grid=(domains, groups), out_shape=jax.Shap...]
    ppermute x11, waiting for transfers between devices: 6.73 us -> 5.41 us  [exchange(): return lax.ppermute(shard, axis, [(i, i ^ mask) for i in range(devices)])]
    pallas_call x1, Pallas kernels: 22.5 us -> 21.8 us  [run_lanczos(): pl.pallas_call(kernel, out_shape=(jax.ShapeDtypeStruct((STEPS, states, st...]
  transfers between devices with their start and end apart: 11 -> 11, of which waited for: 7 -> 4; matrix products, arithmetic and copies ran while one was open for 2% -> 4% of each run, Pallas kernels for 26% -> 23%
where the time goes in v3:
time: 60.6 us; the launch traced here: 60.2 us
  Pallas kernels  36.9 us (61%)
  starting transfers between devices  13.9 us (23%)
  waiting for transfers between devices  5.41 us (9%)
  local copies, waits for them, and re-layouts  2.42 us (4%)
  between operations  0.93 us (2%)
  other arithmetic  0.73 us (1%)
    pallas_call x1, Pallas kernels, run_lanczos(): pl.pallas_call(kernel, out_shape=(jax.ShapeDtypeStruct((STEPS, states, st...  21.8 us
    ppermute x11, starting transfers between devices, exchange(): return lax.ppermute(shard, axis, [(i, i ^ mask) for i in range(devices)])  13.9 us
    pallas_call x1, Pallas kernels, run_network(): pl.pallas_call(network_kernel, grid=(domains, groups), out_shape=jax.Shap...  13.6 us
    ppermute x11, waiting for transfers between devices, exchange(): return lax.ppermute(shard, axis, [(i, i ^ mask) for i in range(devices)])  5.41 us
    pallas_call x1, Pallas kernels, run_lanes(): pl.pallas_call(lanes_kernel, out_shape=jax.ShapeDtypeStruct((2, distance....  1.54 us
  transfers between devices with their start and end apart: 11, of which 4 were waited for; matrix products, arithmetic and copies ran while one was open for 4% of the time, Pallas kernels for 23%

profile of v3, /device:TPU:0, one launch (start us, length us, event | category | flops | bytes accessed | tf_op | source)
XLA Modules:
  0.0 60.2 jit_solution(4763029417065056286)
XLA Ops:
  0.6 1.5 %slot_lanes.1 = f32[2,16,128]{2,1,0:T(8,128)} custom-call(f32[16,32]{1,0:T(8,128)} %bitcast.14, s32[16,32]{1,0:T(8,128)} %bitcast.15, s32[1,32]{1,0:T(1,128)} %bitcast.16), custom_call_target="tpu_custom_call" | custom-call | tf_op jit(solution)/shard_map/slot_lanes/pallas_call | solution.py:246
  2.2 0.5 collective-permute-start
  2.6 0.9 %dynamic-slice_bitcast_fusion = f32[13,16,128]{2,1,0:T(8,128)S(1)} fusion(f32[32,13,128]{2,0,1:T(8,128)} %param.21, s32[]{:T(128)S(6)} %select_n.3), kind=kLoop, calls=%fused_computation | loop fusion | bytes 212996 | tf_op jit(solution)/shard_map/dynamic_slice | solution.py:706
  3.5 4.6 %collective-permute-start.7 = (f32[13,16,128]{2,1,0:T(8,128)S(1)}, f32[13,16,128]{2,1,0:T(8,128)S(1)}, u32[]{:S(2)}, u32[]{:S(2)}) collective-permute-start(f32[13,16,128]{2,1,0:T(8,128)S(1)} %dynamic-slice_bitcast_fusion), channel_id=1, source_target_pairs={{0,12},{4,8},{8,4},{12,0},{1,13},{5,9},{9,5},{13,1},{2,14},{6,10},... | collective-permute-start | bytes 319496 | tf_op jit(solution)/shard_map/ppermute | solution.py:664
  8.1 0.0 collective-permute-start.6
  8.1 0.6 %collective-permute-start.5 = (f32[13,16,128]{2,1,0:T(8,128)S(1)}, f32[13,16,128]{2,1,0:T(8,128)S(1)}, u32[]{:S(2)}, u32[]{:S(2)}) collective-permute-start(f32[13,16,128]{2,1,0:T(8,128)S(1)} %dynamic-slice_bitcast_fusion), channel_id=1, source_target_pairs={{0,4},{4,0},{8,12},{12,8},{1,5},{5,1},{9,13},{13,9},{2,6},{6,2},{1... | collective-permute-start | bytes 319496 | tf_op jit(solution)/shard_map/ppermute | solution.py:664
  8.8 0.0 collective-permute-done
  8.8 0.7 %add.9 = f32[2,16,128]{2,1,0:T(8,128)S(1)} add(f32[2,16,128]{2,1,0:T(8,128)} %slot_lanes.1, f32[2,16,128]{2,1,0:T(8,128)S(1)} %collective-permute-done) | non-fusion elementwise | flops 4096 | bytes 49152 | tf_op jit(solution)/shard_map/add | solution.py:708
  9.5 1.7 %collective-permute-start.1 = (f32[2,16,128]{2,1,0:T(8,128)S(1)}, f32[2,16,128]{2,1,0:T(8,128)S(1)}, u32[]{:S(2)}, u32[]{:S(2)}) collective-permute-start(f32[2,16,128]{2,1,0:T(8,128)S(1)} %add.9), channel_id=1, source_target_pairs={{0,2},{2,0},{1,3},{3,1},{4,6},{6,4},{5,7},{7,5},{8,10},{10,8},{9,1... | collective-permute-start | bytes 49160 | tf_op jit(solution)/shard_map/ppermute | solution.py:664
  11.1 0.7 %fusion = (f32[32,128]{1,0:T(8,128)S(1)}, f32[32,128]{1,0:T(8,128)S(1)}) fusion(bf16[32,256]{1,0:T(8,128)(2,1)} %param.11), kind=kLoop, calls=%fused_computation.2 | loop fusion | bytes 65536 | tf_op jit(solution)/shard_map/slice | solution.py:711
  11.9 1.4 %collective-permute-done.1 = f32[2,16,128]{2,1,0:T(8,128)S(1)} collective-permute-done((f32[2,16,128]{2,1,0:T(8,128)S(1)}, f32[2,16,128]{2,1,0:T(8,128)S(1)}, u32[]{:S(2)}, u32[]{:S(2)}) %collective-permute-start.1) | collective-permute-done | bytes 16416 | tf_op jit(solution)/shard_map/ppermute | solution.py:664
  13.2 0.0 copy-start.6
  13.3 1.5 %collective-permute-start.2 = (f32[96,128]{1,0:T(8,128)S(1)}, f32[96,128]{1,0:T(8,128)S(1)}, u32[]{:S(2)}, u32[]{:S(2)}) collective-permute-start(f32[96,128]{1,0:T(8,128)S(1)} %pad_maximum_fusion.pack0), channel_id=1, source_target_pairs={{0,4},{4,0},{8,12},{12,8},{1,5},{5,1},{9,13},{13,9},{2,6},{6,2},{1... | collective-permute-start | bytes 147464 | tf_op jit(solution)/shard_map/ppermute | solution.py:664
  14.7 2.9 %collective-permute-start.3 = (f32[96,128]{1,0:T(8,128)S(1)}, f32[96,128]{1,0:T(8,128)S(1)}, u32[]{:S(2)}, u32[]{:S(2)}) collective-permute-start(f32[96,128]{1,0:T(8,128)S(1)} %pad_maximum_fusion.pack0), channel_id=1, source_target_pairs={{0,8},{4,12},{8,0},{12,4},{1,9},{5,13},{9,1},{13,5},{2,10},{6,14},... | collective-permute-start | bytes 147464 | tf_op jit(solution)/shard_map/ppermute | solution.py:664
  17.6 0.7 %collective-permute-done.2.pack1 = f32[96,128]{1,0:T(8,128)S(1)} collective-permute-done((f32[96,128]{1,0:T(8,128)S(1)}, f32[96,128]{1,0:T(8,128)S(1)}, u32[]{:S(2)}, u32[]{:S(2)}) %collective-permute-start.2) | collective-permute-done | bytes 49184 | tf_op jit(solution)/shard_map/ppermute | solution.py:664
  18.3 0.0 copy-start.7
  18.3 1.6 %collective-permute-start.4 = (f32[96,128]{1,0:T(8,128)S(1)}, f32[96,128]{1,0:T(8,128)S(1)}, u32[]{:S(2)}, u32[]{:S(2)}) collective-permute-start(f32[96,128]{1,0:T(8,128)S(1)} %collective-permute-done.2.pack1), channel_id=1, source_target_pairs={{0,8},{4,12},{8,0},{12,4},{1,9},{5,13},{9,1},{13,5},{2,10},{6,14},... | collective-permute-start | bytes 147464 | tf_op jit(solution)/shard_map/ppermute | solution.py:664
  20.0 0.3 collective-permute-done.3.pack2
  20.2 0.0 copy-start.8
  20.2 0.0 collective-permute-done.7.refs_3_
  20.2 0.0 copy-start
  20.2 0.0 collective-permute-done.6.refs_2_
  20.2 0.0 copy-start.1
  20.3 0.0 collective-permute-done.5.refs_1_
  20.3 0.0 copy-start.2
  20.3 3.1 %collective-permute-done.4.pack3 = f32[96,128]{1,0:T(8,128)S(1)} collective-permute-done((f32[96,128]{1,0:T(8,128)S(1)}, f32[96,128]{1,0:T(8,128)S(1)}, u32[]{:S(2)}, u32[]{:S(2)}) %collective-permute-start.4) | collective-permute-done | bytes 49184 | tf_op jit(solution)/shard_map/ppermute | solution.py:664
  23.3 0.0 copy-start.9
  23.3 0.0 collective-permute-start.8
  23.3 0.5 collective-permute-start.9
  23.9 0.0 collective-permute-start.10
  23.9 0.0 copy-done.6
  23.9 0.0 copy-done.7
  23.9 0.0 copy-done.8
  23.9 0.1 copy-done.9
  24.0 13.6 %pair_network.1 = bf16[13,128,1664]{2,1,0:T(8,128)(2,1)} custom-call(f32[96,128]{1,0:T(8,128)} %copy-done.6, f32[96,128]{1,0:T(8,128)} %copy-done.7, f32[96,128]{1,0:T(8,128)} %copy-done.8, f32[96,128]{1,0:T(8,128)} %copy-done.9, bf16[256,256]{1,0:T(8,128)(2,1)} %w_source.1, bf16[256,256]{1,0:T(8,128)(2,1)} %w_target.1, bf16[128,256]{1,0:T(8,128)(2,1)} %w_radial.1, ...), custom_call_target="tpu_custom_call" | custom-call | flops 6000000000 | bytes 8000000 | tf_op jit(solution)/shard_map/pair_network/pallas_call | solution.py:398
  37.5 0.0 copy-done
  37.5 0.0 copy-done.1
  37.5 0.0 copy-done.2
  37.5 0.0 collective-permute-done.8.refs_4_
  37.6 0.0 copy-start.3
  37.6 0.0 collective-permute-done.9.refs_5_
  37.6 0.0 copy-start.4
  37.6 0.0 collective-permute-done.10.refs_6_
  37.6 0.0 copy-start.5
  37.6 0.6 copy-done.3
  38.2 0.0 copy-done.4
  38.2 0.1 copy-done.5
  38.3 21.8 %block_lanczos.1 = (f32[2,128,128]{2,1,0:T(8,128)}, f32[2,128,128]{2,1,0:T(8,128)}, f32[13,32,128]{2,1,0:T(8,128)}) custom-call(f32[13,32,128]{2,1,0:T(8,128)} %bitcast.12, f32[13,16,128]{2,1,0:T(8,128)} %copy-done.2, f32[13,16,128]{2,1,0:T(8,128)} %copy-done.1, f32[13,16,128]{2,1,0:T(8,128)} %copy-done, f32[13,16,128]{2,1,0:T(8,128)} %copy-done.3, ...), custom_call_target="tpu_custom_call" | custom-call | tf_op jit(solution)/shard_map/block_lanczos/pallas_call | solution.py:640
  (2 shorter events, 0.0 us)
Async XLA Ops:
  2.2 6.6 %collective-permute-start = (f32[2,16,128]{2,1,0:T(8,128)}, f32[2,16,128]{2,1,0:T(8,128)S(1)}, u32[]{:S(2)}, u32[]{:S(2)}) collective-permute-start(f32[2,16,128]{2,1,0:T(8,128)} %slot_lanes.1), channel_id=1, source_target_pairs={{0,1},{1,0},{2,3},{3,2},{4,5},{5,4},{6,7},{7,6},{8,9},{9,8},{10,11... | collective-permute-start | bytes 49160 | tf_op jit(solution)/shard_map/ppermute | solution.py:664
  3.5 16.7 %collective-permute-start.7 = (f32[13,16,128]{2,1,0:T(8,128)S(1)}, f32[13,16,128]{2,1,0:T(8,128)S(1)}, u32[]{:S(2)}, u32[]{:S(2)}) collective-permute-start(f32[13,16,128]{2,1,0:T(8,128)S(1)} %dynamic-slice_bitcast_fusion), channel_id=1, source_target_pairs={{0,12},{4,8},{8,4},{12,0},{1,13},{5,9},{9,5},{13,1},{2,14},{6,10},... | collective-permute-start | bytes 319496 | tf_op jit(solution)/shard_map/ppermute | solution.py:664
  8.1 12.1 %collective-permute-start.6 = (f32[13,16,128]{2,1,0:T(8,128)S(1)}, f32[13,16,128]{2,1,0:T(8,128)S(1)}, u32[]{:S(2)}, u32[]{:S(2)}) collective-permute-start(f32[13,16,128]{2,1,0:T(8,128)S(1)} %dynamic-slice_bitcast_fusion), channel_id=1, source_target_pairs={{0,8},{4,12},{8,0},{12,4},{1,9},{5,13},{9,1},{13,5},{2,10},{6,14},... | collective-permute-start | bytes 319496 | tf_op jit(solution)/shard_map/ppermute | solution.py:664
  8.1 12.1 %collective-permute-start.5 = (f32[13,16,128]{2,1,0:T(8,128)S(1)}, f32[13,16,128]{2,1,0:T(8,128)S(1)}, u32[]{:S(2)}, u32[]{:S(2)}) collective-permute-start(f32[13,16,128]{2,1,0:T(8,128)S(1)} %dynamic-slice_bitcast_fusion), channel_id=1, source_target_pairs={{0,4},{4,0},{8,12},{12,8},{1,5},{5,1},{9,13},{13,9},{2,6},{6,2},{1... | collective-permute-start | bytes 319496 | tf_op jit(solution)/shard_map/ppermute | solution.py:664
  9.5 3.7 %collective-permute-start.1 = (f32[2,16,128]{2,1,0:T(8,128)S(1)}, f32[2,16,128]{2,1,0:T(8,128)S(1)}, u32[]{:S(2)}, u32[]{:S(2)}) collective-permute-start(f32[2,16,128]{2,1,0:T(8,128)S(1)} %add.9), channel_id=1, source_target_pairs={{0,2},{2,0},{1,3},{3,1},{4,6},{6,4},{5,7},{7,5},{8,10},{10,8},{9,1... | collective-permute-start | bytes 49160 | tf_op jit(solution)/shard_map/ppermute | solution.py:664
  13.2 10.6 %copy-start.6 = (f32[96,128]{1,0:T(8,128)}, f32[96,128]{1,0:T(8,128)S(1)}, u32[]{:S(2)}) copy-start(f32[96,128]{1,0:T(8,128)S(1)} %pad_maximum_fusion.pack0) | copy-start | bytes 147460
  13.3 5.1 %collective-permute-start.2 = (f32[96,128]{1,0:T(8,128)S(1)}, f32[96,128]{1,0:T(8,128)S(1)}, u32[]{:S(2)}, u32[]{:S(2)}) collective-permute-start(f32[96,128]{1,0:T(8,128)S(1)} %pad_maximum_fusion.pack0), channel_id=1, source_target_pairs={{0,4},{4,0},{8,12},{12,8},{1,5},{5,1},{9,13},{13,9},{2,6},{6,2},{1... | collective-permute-start | bytes 147464 | tf_op jit(solution)/shard_map/ppermute | solution.py:664
  14.7 5.5 %collective-permute-start.3 = (f32[96,128]{1,0:T(8,128)S(1)}, f32[96,128]{1,0:T(8,128)S(1)}, u32[]{:S(2)}, u32[]{:S(2)}) collective-permute-start(f32[96,128]{1,0:T(8,128)S(1)} %pad_maximum_fusion.pack0), channel_id=1, source_target_pairs={{0,8},{4,12},{8,0},{12,4},{1,9},{5,13},{9,1},{13,5},{2,10},{6,14},... | collective-permute-start | bytes 147464 | tf_op jit(solution)/shard_map/ppermute | solution.py:664
  18.3 5.5 %copy-start.7 = (f32[96,128]{1,0:T(8,128)}, f32[96,128]{1,0:T(8,128)S(1)}, u32[]{:S(2)}) copy-start(f32[96,128]{1,0:T(8,128)S(1)} %collective-permute-done.2.pack1) | copy-start | bytes 147460
  18.3 5.0 %collective-permute-start.4 = (f32[96,128]{1,0:T(8,128)S(1)}, f32[96,128]{1,0:T(8,128)S(1)}, u32[]{:S(2)}, u32[]{:S(2)}) collective-permute-start(f32[96,128]{1,0:T(8,128)S(1)} %collective-permute-done.2.pack1), channel_id=1, source_target_pairs={{0,8},{4,12},{8,0},{12,4},{1,9},{5,13},{9,1},{13,5},{2,10},{6,14},... | collective-permute-start | bytes 147464 | tf_op jit(solution)/shard_map/ppermute | solution.py:664
  20.2 3.6 %copy-start.8 = (f32[96,128]{1,0:T(8,128)}, f32[96,128]{1,0:T(8,128)S(1)}, u32[]{:S(2)}) copy-start(f32[96,128]{1,0:T(8,128)S(1)} %collective-permute-done.3.pack2) | copy-start | bytes 147460
  20.2 17.3 %copy-start = (f32[13,16,128]{2,1,0:T(8,128)}, f32[13,16,128]{2,1,0:T(8,128)S(1)}, u32[]{:S(2)}) copy-start(f32[13,16,128]{2,1,0:T(8,128)S(1)} %collective-permute-done.7.refs_3_) | copy-start | bytes 319492
  20.2 17.3 %copy-start.1 = (f32[13,16,128]{2,1,0:T(8,128)}, f32[13,16,128]{2,1,0:T(8,128)S(1)}, u32[]{:S(2)}) copy-start(f32[13,16,128]{2,1,0:T(8,128)S(1)} %collective-permute-done.6.refs_2_) | copy-start | bytes 319492
  20.3 17.3 %copy-start.2 = (f32[13,16,128]{2,1,0:T(8,128)}, f32[13,16,128]{2,1,0:T(8,128)S(1)}, u32[]{:S(2)}) copy-start(f32[13,16,128]{2,1,0:T(8,128)S(1)} %collective-permute-done.5.refs_1_) | copy-start | bytes 319492
  23.3 0.6 %copy-start.9 = (f32[96,128]{1,0:T(8,128)}, f32[96,128]{1,0:T(8,128)S(1)}, u32[]{:S(2)}) copy-start(f32[96,128]{1,0:T(8,128)S(1)} %collective-permute-done.4.pack3) | copy-start | bytes 147460
  23.3 14.2 %collective-permute-start.8 = (f32[13,16,128]{2,1,0:T(8,128)S(1)}, f32[13,16,128]{2,1,0:T(8,128)S(1)}, u32[]{:S(2)}, u32[]{:S(2)}) collective-permute-start(f32[13,16,128]{2,1,0:T(8,128)S(1)} %collective-permute-done.5.refs_1_), channel_id=1, source_target_pairs={{0,1},{1,0},{2,3},{3,2},{4,5},{5,4},{6,7},{7,6},{8,9},{9,8},{10,11... | collective-permute-start | bytes 319496 | tf_op jit(solution)/shard_map/ppermute | solution.py:664
  23.3 14.2 %collective-permute-start.9 = (f32[13,16,128]{2,1,0:T(8,128)S(1)}, f32[13,16,128]{2,1,0:T(8,128)S(1)}, u32[]{:S(2)}, u32[]{:S(2)}) collective-permute-start(f32[13,16,128]{2,1,0:T(8,128)S(1)} %collective-permute-done.6.refs_2_), channel_id=1, source_target_pairs={{0,1},{1,0},{2,3},{3,2},{4,5},{5,4},{6,7},{7,6},{8,9},{9,8},{10,11... | collective-permute-start | bytes 319496 | tf_op jit(solution)/shard_map/ppermute | solution.py:664
  23.9 13.7 %collective-permute-start.10 = (f32[13,16,128]{2,1,0:T(8,128)S(1)}, f32[13,16,128]{2,1,0:T(8,128)S(1)}, u32[]{:S(2)}, u32[]{:S(2)}) collective-permute-start(f32[13,16,128]{2,1,0:T(8,128)S(1)} %collective-permute-done.7.refs_3_), channel_id=1, source_target_pairs={{0,1},{1,0},{2,3},{3,2},{4,5},{5,4},{6,7},{7,6},{8,9},{9,8},{10,11... | collective-permute-start | bytes 319496 | tf_op jit(solution)/shard_map/ppermute | solution.py:664
  37.6 0.6 %copy-start.3 = (f32[13,16,128]{2,1,0:T(8,128)}, f32[13,16,128]{2,1,0:T(8,128)S(1)}, u32[]{:S(2)}) copy-start(f32[13,16,128]{2,1,0:T(8,128)S(1)} %collective-permute-done.8.refs_4_) | copy-start | bytes 319492
  37.6 0.7 %copy-start.4 = (f32[13,16,128]{2,1,0:T(8,128)}, f32[13,16,128]{2,1,0:T(8,128)S(1)}, u32[]{:S(2)}) copy-start(f32[13,16,128]{2,1,0:T(8,128)S(1)} %collective-permute-done.9.refs_5_) | copy-start | bytes 319492
  37.6 0.7 %copy-start.5 = (f32[13,16,128]{2,1,0:T(8,128)}, f32[13,16,128]{2,1,0:T(8,128)S(1)}, u32[]{:S(2)}) copy-start(f32[13,16,128]{2,1,0:T(8,128)S(1)} %collective-permute-done.10.refs_6_) | copy-start | bytes 319492

commit v4 on v3

--- a/solution.py
+++ b/solution.py
@@ -476,8 +476,6 @@
                 done = beside[p + 1][r]
                 for k in range(PANEL):
                     following[k] = following[k] - done * spread_rows(done, k, PANEL)
-        if p < len(fill):
-            fill[p]()
         top = unit[0] * spread_rows(work[p], 0, PANEL)
         side = unit[0] * spread_rows(extra[p], 0, PANEL)
         for c in range(1, PANEL):
@@ -496,11 +494,15 @@
                     extra[q] = extra[q] - beside[q][c] * sides[c]
             if p + 1 + NEAR < count:
                 change = outer_change(top, side)
+                if p < len(fill):
+                    fill[p]()
                 for q in range(p + 1 + NEAR, count):
                     rows = slice(q * PANEL, (q + 1) * PANEL)
                     work[q] = work[q] - change[rows, :order]
                     extra[q] = extra[q] - change[rows, order:]
             block = following
+    for run in fill[count - 1 - NEAR :]:
+        run()
     return jnp.concatenate(upper, axis=0), jnp.concatenate(inverse, axis=0)
 
 
@@ -557,8 +559,8 @@
         flat[:, :states] = pieces[0]
         flat[:, states:] = pieces[1]
 
-    chunk = 208
-    width = 256
+    chunk = 416
+    width = 512
 
     def forward(start):
         def run():
@@ -600,8 +602,10 @@
     pieces = split(whole(xs))
     set_flat(pieces)
     gram = own_gram(pieces)
+    factor, inverse = factor_panels(gram)
     copy.wait()
-    factor, inverse = factor_panels(gram, fill)
+    for run in fill:
+        run()
     inverse = split(inverse)
     first = side(split(times_turned(flat[...], inverse)))
     qs[...] = first

time: 60.6 us -> 58.6 us (0.967)
  Pallas kernels: 36.9 us -> 34.9 us
    pallas_call x1, Pallas kernels: 21.8 us -> 19.8 us  [run_lanczos(): pl.pallas_call(kernel, out_shape=(jax.ShapeDtypeStruct((STEPS, states, st...]
where the time goes in v4:
time: 58.6 us; the launch traced here: 58.3 us
  Pallas kernels  34.9 us (60%)
  starting transfers between devices  13.9 us (24%)
  waiting for transfers between devices  5.41 us (9%)
  local copies, waits for them, and re-layouts  2.42 us (4%)
  between operations  0.93 us (2%)
  other arithmetic  0.73 us (1%)
    pallas_call x1, Pallas kernels, run_lanczos(): pl.pallas_call(kernel, out_shape=(jax.ShapeDtypeStruct((STEPS, states, st...  19.8 us
    ppermute x11, starting transfers between devices, exchange(): return lax.ppermute(shard, axis, [(i, i ^ mask) for i in range(devices)])  13.9 us
    pallas_call x1, Pallas kernels, run_network(): pl.pallas_call(network_kernel, grid=(domains, groups), out_shape=jax.Shap...  13.6 us
    ppermute x11, waiting for transfers between devices, exchange(): return lax.ppermute(shard, axis, [(i, i ^ mask) for i in range(devices)])  5.41 us
    pallas_call x1, Pallas kernels, run_lanes(): pl.pallas_call(lanes_kernel, out_shape=jax.ShapeDtypeStruct((2, distance....  1.54 us
  transfers between devices with their start and end apart: 11, of which 4 were waited for; matrix products, arithmetic and copies ran while one was open for 4% of the time, Pallas kernels for 23%

profile of v4, /device:TPU:0, one launch (start us, length us, event | category | flops | bytes accessed | tf_op | source)
XLA Modules:
  0.0 58.3 jit_solution(12060899344384910114)
XLA Ops:
  0.6 1.5 %slot_lanes.1 = f32[2,16,128]{2,1,0:T(8,128)} custom-call(f32[16,32]{1,0:T(8,128)} %bitcast.14, s32[16,32]{1,0:T(8,128)} %bitcast.15, s32[1,32]{1,0:T(1,128)} %bitcast.16), custom_call_target="tpu_custom_call" | custom-call | tf_op jit(solution)/shard_map/slot_lanes/pallas_call | solution.py:246
  2.2 0.5 collective-permute-start
  2.6 0.9 %dynamic-slice_bitcast_fusion = f32[13,16,128]{2,1,0:T(8,128)S(1)} fusion(f32[32,13,128]{2,0,1:T(8,128)} %param.21, s32[]{:T(128)S(6)} %select_n.3), kind=kLoop, calls=%fused_computation | loop fusion | bytes 212996 | tf_op jit(solution)/shard_map/dynamic_slice | solution.py:710
  3.5 4.6 %collective-permute-start.7 = (f32[13,16,128]{2,1,0:T(8,128)S(1)}, f32[13,16,128]{2,1,0:T(8,128)S(1)}, u32[]{:S(2)}, u32[]{:S(2)}) collective-permute-start(f32[13,16,128]{2,1,0:T(8,128)S(1)} %dynamic-slice_bitcast_fusion), channel_id=1, source_target_pairs={{0,12},{4,8},{8,4},{12,0},{1,13},{5,9},{9,5},{13,1},{2,14},{6,10},... | collective-permute-start | bytes 319496 | tf_op jit(solution)/shard_map/ppermute | solution.py:668
  8.1 0.0 collective-permute-start.6
  8.1 0.6 %collective-permute-start.5 = (f32[13,16,128]{2,1,0:T(8,128)S(1)}, f32[13,16,128]{2,1,0:T(8,128)S(1)}, u32[]{:S(2)}, u32[]{:S(2)}) collective-permute-start(f32[13,16,128]{2,1,0:T(8,128)S(1)} %dynamic-slice_bitcast_fusion), channel_id=1, source_target_pairs={{0,4},{4,0},{8,12},{12,8},{1,5},{5,1},{9,13},{13,9},{2,6},{6,2},{1... | collective-permute-start | bytes 319496 | tf_op jit(solution)/shard_map/ppermute | solution.py:668
  8.8 0.0 collective-permute-done
  8.8 0.7 %add.9 = f32[2,16,128]{2,1,0:T(8,128)S(1)} add(f32[2,16,128]{2,1,0:T(8,128)} %slot_lanes.1, f32[2,16,128]{2,1,0:T(8,128)S(1)} %collective-permute-done) | non-fusion elementwise | flops 4096 | bytes 49152 | tf_op jit(solution)/shard_map/add | solution.py:712
  9.5 1.7 %collective-permute-start.1 = (f32[2,16,128]{2,1,0:T(8,128)S(1)}, f32[2,16,128]{2,1,0:T(8,128)S(1)}, u32[]{:S(2)}, u32[]{:S(2)}) collective-permute-start(f32[2,16,128]{2,1,0:T(8,128)S(1)} %add.9), channel_id=1, source_target_pairs={{0,2},{2,0},{1,3},{3,1},{4,6},{6,4},{5,7},{7,5},{8,10},{10,8},{9,1... | collective-permute-start | bytes 49160 | tf_op jit(solution)/shard_map/ppermute | solution.py:668
  11.1 0.7 %fusion = (f32[32,128]{1,0:T(8,128)S(1)}, f32[32,128]{1,0:T(8,128)S(1)}) fusion(bf16[32,256]{1,0:T(8,128)(2,1)} %param.11), kind=kLoop, calls=%fused_computation.2 | loop fusion | bytes 65536 | tf_op jit(solution)/shard_map/slice | solution.py:715
  11.9 1.4 %collective-permute-done.1 = f32[2,16,128]{2,1,0:T(8,128)S(1)} collective-permute-done((f32[2,16,128]{2,1,0:T(8,128)S(1)}, f32[2,16,128]{2,1,0:T(8,128)S(1)}, u32[]{:S(2)}, u32[]{:S(2)}) %collective-permute-start.1) | collective-permute-done | bytes 16416 | tf_op jit(solution)/shard_map/ppermute | solution.py:668
  13.2 0.0 copy-start.6
  13.3 1.5 %collective-permute-start.2 = (f32[96,128]{1,0:T(8,128)S(1)}, f32[96,128]{1,0:T(8,128)S(1)}, u32[]{:S(2)}, u32[]{:S(2)}) collective-permute-start(f32[96,128]{1,0:T(8,128)S(1)} %pad_maximum_fusion.pack0), channel_id=1, source_target_pairs={{0,4},{4,0},{8,12},{12,8},{1,5},{5,1},{9,13},{13,9},{2,6},{6,2},{1... | collective-permute-start | bytes 147464 | tf_op jit(solution)/shard_map/ppermute | solution.py:668
  14.7 2.9 %collective-permute-start.3 = (f32[96,128]{1,0:T(8,128)S(1)}, f32[96,128]{1,0:T(8,128)S(1)}, u32[]{:S(2)}, u32[]{:S(2)}) collective-permute-start(f32[96,128]{1,0:T(8,128)S(1)} %pad_maximum_fusion.pack0), channel_id=1, source_target_pairs={{0,8},{4,12},{8,0},{12,4},{1,9},{5,13},{9,1},{13,5},{2,10},{6,14},... | collective-permute-start | bytes 147464 | tf_op jit(solution)/shard_map/ppermute | solution.py:668
  17.6 0.7 %collective-permute-done.2.pack1 = f32[96,128]{1,0:T(8,128)S(1)} collective-permute-done((f32[96,128]{1,0:T(8,128)S(1)}, f32[96,128]{1,0:T(8,128)S(1)}, u32[]{:S(2)}, u32[]{:S(2)}) %collective-permute-start.2) | collective-permute-done | bytes 49184 | tf_op jit(solution)/shard_map/ppermute | solution.py:668
  18.3 0.0 copy-start.7
  18.3 1.6 %collective-permute-start.4 = (f32[96,128]{1,0:T(8,128)S(1)}, f32[96,128]{1,0:T(8,128)S(1)}, u32[]{:S(2)}, u32[]{:S(2)}) collective-permute-start(f32[96,128]{1,0:T(8,128)S(1)} %collective-permute-done.2.pack1), channel_id=1, source_target_pairs={{0,8},{4,12},{8,0},{12,4},{1,9},{5,13},{9,1},{13,5},{2,10},{6,14},... | collective-permute-start | bytes 147464 | tf_op jit(solution)/shard_map/ppermute | solution.py:668
  20.0 0.3 collective-permute-done.3.pack2
  20.2 0.0 copy-start.8
  20.2 0.0 collective-permute-done.7.refs_3_
  20.2 0.0 copy-start
  20.2 0.0 collective-permute-done.6.refs_2_
  20.2 0.0 copy-start.1
  20.3 0.0 collective-permute-done.5.refs_1_
  20.3 0.0 copy-start.2
  20.3 3.1 %collective-permute-done.4.pack3 = f32[96,128]{1,0:T(8,128)S(1)} collective-permute-done((f32[96,128]{1,0:T(8,128)S(1)}, f32[96,128]{1,0:T(8,128)S(1)}, u32[]{:S(2)}, u32[]{:S(2)}) %collective-permute-start.4) | collective-permute-done | bytes 49184 | tf_op jit(solution)/shard_map/ppermute | solution.py:668
  23.3 0.0 copy-start.9
  23.3 0.0 collective-permute-start.8
  23.3 0.5 collective-permute-start.9
  23.9 0.0 collective-permute-start.10
  23.9 0.0 copy-done.6
  23.9 0.0 copy-done.7
  23.9 0.0 copy-done.8
  23.9 0.1 copy-done.9
  24.0 13.6 %pair_network.1 = bf16[13,128,1664]{2,1,0:T(8,128)(2,1)} custom-call(f32[96,128]{1,0:T(8,128)} %copy-done.6, f32[96,128]{1,0:T(8,128)} %copy-done.7, f32[96,128]{1,0:T(8,128)} %copy-done.8, f32[96,128]{1,0:T(8,128)} %copy-done.9, bf16[256,256]{1,0:T(8,128)(2,1)} %w_source.1, bf16[256,256]{1,0:T(8,128)(2,1)} %w_target.1, bf16[128,256]{1,0:T(8,128)(2,1)} %w_radial.1, ...), custom_call_target="tpu_custom_call" | custom-call | flops 6000000000 | bytes 8000000 | tf_op jit(solution)/shard_map/pair_network/pallas_call | solution.py:398
  37.5 0.0 copy-done
  37.5 0.0 copy-done.1
  37.5 0.0 copy-done.2
  37.5 0.0 collective-permute-done.8.refs_4_
  37.6 0.0 copy-start.3
  37.6 0.0 collective-permute-done.9.refs_5_
  37.6 0.0 copy-start.4
  37.6 0.0 collective-permute-done.10.refs_6_
  37.6 0.0 copy-start.5
  37.6 0.6 %copy-done.3 = f32[13,16,128]{2,1,0:T(8,128)} copy-done((f32[13,16,128]{2,1,0:T(8,128)}, f32[13,16,128]{2,1,0:T(8,128)S(1)}, u32[]{:S(2)}) %copy-start.3) | copy-done | bytes 106520
  38.2 0.0 copy-done.4
  38.2 0.1 copy-done.5
  38.3 19.8 %block_lanczos.1 = (f32[2,128,128]{2,1,0:T(8,128)}, f32[2,128,128]{2,1,0:T(8,128)}, f32[13,32,128]{2,1,0:T(8,128)}) custom-call(f32[13,32,128]{2,1,0:T(8,128)} %bitcast.12, f32[13,16,128]{2,1,0:T(8,128)} %copy-done.2, f32[13,16,128]{2,1,0:T(8,128)} %copy-done.1, f32[13,16,128]{2,1,0:T(8,128)} %copy-done, f32[13,16,128]{2,1,0:T(8,128)} %copy-done.3, ...), custom_call_target="tpu_custom_call" | custom-call | tf_op jit(solution)/shard_map/block_lanczos/pallas_call | solution.py:644
  (2 shorter events, 0.0 us)
Async XLA Ops:
  2.2 6.6 %collective-permute-start = (f32[2,16,128]{2,1,0:T(8,128)}, f32[2,16,128]{2,1,0:T(8,128)S(1)}, u32[]{:S(2)}, u32[]{:S(2)}) collective-permute-start(f32[2,16,128]{2,1,0:T(8,128)} %slot_lanes.1), channel_id=1, source_target_pairs={{0,1},{1,0},{2,3},{3,2},{4,5},{5,4},{6,7},{7,6},{8,9},{9,8},{10,11... | collective-permute-start | bytes 49160 | tf_op jit(solution)/shard_map/ppermute | solution.py:668
  3.5 16.7 %collective-permute-start.7 = (f32[13,16,128]{2,1,0:T(8,128)S(1)}, f32[13,16,128]{2,1,0:T(8,128)S(1)}, u32[]{:S(2)}, u32[]{:S(2)}) collective-permute-start(f32[13,16,128]{2,1,0:T(8,128)S(1)} %dynamic-slice_bitcast_fusion), channel_id=1, source_target_pairs={{0,12},{4,8},{8,4},{12,0},{1,13},{5,9},{9,5},{13,1},{2,14},{6,10},... | collective-permute-start | bytes 319496 | tf_op jit(solution)/shard_map/ppermute | solution.py:668
  8.1 12.1 %collective-permute-start.6 = (f32[13,16,128]{2,1,0:T(8,128)S(1)}, f32[13,16,128]{2,1,0:T(8,128)S(1)}, u32[]{:S(2)}, u32[]{:S(2)}) collective-permute-start(f32[13,16,128]{2,1,0:T(8,128)S(1)} %dynamic-slice_bitcast_fusion), channel_id=1, source_target_pairs={{0,8},{4,12},{8,0},{12,4},{1,9},{5,13},{9,1},{13,5},{2,10},{6,14},... | collective-permute-start | bytes 319496 | tf_op jit(solution)/shard_map/ppermute | solution.py:668
  8.1 12.1 %collective-permute-start.5 = (f32[13,16,128]{2,1,0:T(8,128)S(1)}, f32[13,16,128]{2,1,0:T(8,128)S(1)}, u32[]{:S(2)}, u32[]{:S(2)}) collective-permute-start(f32[13,16,128]{2,1,0:T(8,128)S(1)} %dynamic-slice_bitcast_fusion), channel_id=1, source_target_pairs={{0,4},{4,0},{8,12},{12,8},{1,5},{5,1},{9,13},{13,9},{2,6},{6,2},{1... | collective-permute-start | bytes 319496 | tf_op jit(solution)/shard_map/ppermute | solution.py:668
  9.5 3.7 %collective-permute-start.1 = (f32[2,16,128]{2,1,0:T(8,128)S(1)}, f32[2,16,128]{2,1,0:T(8,128)S(1)}, u32[]{:S(2)}, u32[]{:S(2)}) collective-permute-start(f32[2,16,128]{2,1,0:T(8,128)S(1)} %add.9), channel_id=1, source_target_pairs={{0,2},{2,0},{1,3},{3,1},{4,6},{6,4},{5,7},{7,5},{8,10},{10,8},{9,1... | collective-permute-start | bytes 49160 | tf_op jit(solution)/shard_map/ppermute | solution.py:668
  13.2 10.6 %copy-start.6 = (f32[96,128]{1,0:T(8,128)}, f32[96,128]{1,0:T(8,128)S(1)}, u32[]{:S(2)}) copy-start(f32[96,128]{1,0:T(8,128)S(1)} %pad_maximum_fusion.pack0) | copy-start | bytes 147460
  13.3 5.1 %collective-permute-start.2 = (f32[96,128]{1,0:T(8,128)S(1)}, f32[96,128]{1,0:T(8,128)S(1)}, u32[]{:S(2)}, u32[]{:S(2)}) collective-permute-start(f32[96,128]{1,0:T(8,128)S(1)} %pad_maximum_fusion.pack0), channel_id=1, source_target_pairs={{0,4},{4,0},{8,12},{12,8},{1,5},{5,1},{9,13},{13,9},{2,6},{6,2},{1... | collective-permute-start | bytes 147464 | tf_op jit(solution)/shard_map/ppermute | solution.py:668
  14.7 5.5 %collective-permute-start.3 = (f32[96,128]{1,0:T(8,128)S(1)}, f32[96,128]{1,0:T(8,128)S(1)}, u32[]{:S(2)}, u32[]{:S(2)}) collective-permute-start(f32[96,128]{1,0:T(8,128)S(1)} %pad_maximum_fusion.pack0), channel_id=1, source_target_pairs={{0,8},{4,12},{8,0},{12,4},{1,9},{5,13},{9,1},{13,5},{2,10},{6,14},... | collective-permute-start | bytes 147464 | tf_op jit(solution)/shard_map/ppermute | solution.py:668
  18.3 5.5 %copy-start.7 = (f32[96,128]{1,0:T(8,128)}, f32[96,128]{1,0:T(8,128)S(1)}, u32[]{:S(2)}) copy-start(f32[96,128]{1,0:T(8,128)S(1)} %collective-permute-done.2.pack1) | copy-start | bytes 147460
  18.3 5.0 %collective-permute-start.4 = (f32[96,128]{1,0:T(8,128)S(1)}, f32[96,128]{1,0:T(8,128)S(1)}, u32[]{:S(2)}, u32[]{:S(2)}) collective-permute-start(f32[96,128]{1,0:T(8,128)S(1)} %collective-permute-done.2.pack1), channel_id=1, source_target_pairs={{0,8},{4,12},{8,0},{12,4},{1,9},{5,13},{9,1},{13,5},{2,10},{6,14},... | collective-permute-start | bytes 147464 | tf_op jit(solution)/shard_map/ppermute | solution.py:668
  20.2 3.6 %copy-start.8 = (f32[96,128]{1,0:T(8,128)}, f32[96,128]{1,0:T(8,128)S(1)}, u32[]{:S(2)}) copy-start(f32[96,128]{1,0:T(8,128)S(1)} %collective-permute-done.3.pack2) | copy-start | bytes 147460
  20.2 17.3 %copy-start = (f32[13,16,128]{2,1,0:T(8,128)}, f32[13,16,128]{2,1,0:T(8,128)S(1)}, u32[]{:S(2)}) copy-start(f32[13,16,128]{2,1,0:T(8,128)S(1)} %collective-permute-done.7.refs_3_) | copy-start | bytes 319492
  20.2 17.3 %copy-start.1 = (f32[13,16,128]{2,1,0:T(8,128)}, f32[13,16,128]{2,1,0:T(8,128)S(1)}, u32[]{:S(2)}) copy-start(f32[13,16,128]{2,1,0:T(8,128)S(1)} %collective-permute-done.6.refs_2_) | copy-start | bytes 319492
  20.3 17.3 %copy-start.2 = (f32[13,16,128]{2,1,0:T(8,128)}, f32[13,16,128]{2,1,0:T(8,128)S(1)}, u32[]{:S(2)}) copy-start(f32[13,16,128]{2,1,0:T(8,128)S(1)} %collective-permute-done.5.refs_1_) | copy-start | bytes 319492
  23.3 0.6 %copy-start.9 = (f32[96,128]{1,0:T(8,128)}, f32[96,128]{1,0:T(8,128)S(1)}, u32[]{:S(2)}) copy-start(f32[96,128]{1,0:T(8,128)S(1)} %collective-permute-done.4.pack3) | copy-start | bytes 147460
  23.3 14.2 %collective-permute-start.8 = (f32[13,16,128]{2,1,0:T(8,128)S(1)}, f32[13,16,128]{2,1,0:T(8,128)S(1)}, u32[]{:S(2)}, u32[]{:S(2)}) collective-permute-start(f32[13,16,128]{2,1,0:T(8,128)S(1)} %collective-permute-done.5.refs_1_), channel_id=1, source_target_pairs={{0,1},{1,0},{2,3},{3,2},{4,5},{5,4},{6,7},{7,6},{8,9},{9,8},{10,11... | collective-permute-start | bytes 319496 | tf_op jit(solution)/shard_map/ppermute | solution.py:668
  23.3 14.2 %collective-permute-start.9 = (f32[13,16,128]{2,1,0:T(8,128)S(1)}, f32[13,16,128]{2,1,0:T(8,128)S(1)}, u32[]{:S(2)}, u32[]{:S(2)}) collective-permute-start(f32[13,16,128]{2,1,0:T(8,128)S(1)} %collective-permute-done.6.refs_2_), channel_id=1, source_target_pairs={{0,1},{1,0},{2,3},{3,2},{4,5},{5,4},{6,7},{7,6},{8,9},{9,8},{10,11... | collective-permute-start | bytes 319496 | tf_op jit(solution)/shard_map/ppermute | solution.py:668
  23.9 13.7 %collective-permute-start.10 = (f32[13,16,128]{2,1,0:T(8,128)S(1)}, f32[13,16,128]{2,1,0:T(8,128)S(1)}, u32[]{:S(2)}, u32[]{:S(2)}) collective-permute-start(f32[13,16,128]{2,1,0:T(8,128)S(1)} %collective-permute-done.7.refs_3_), channel_id=1, source_target_pairs={{0,1},{1,0},{2,3},{3,2},{4,5},{5,4},{6,7},{7,6},{8,9},{9,8},{10,11... | collective-permute-start | bytes 319496 | tf_op jit(solution)/shard_map/ppermute | solution.py:668
  37.6 0.6 %copy-start.3 = (f32[13,16,128]{2,1,0:T(8,128)}, f32[13,16,128]{2,1,0:T(8,128)S(1)}, u32[]{:S(2)}) copy-start(f32[13,16,128]{2,1,0:T(8,128)S(1)} %collective-permute-done.8.refs_4_) | copy-start | bytes 319492
  37.6 0.7 %copy-start.4 = (f32[13,16,128]{2,1,0:T(8,128)}, f32[13,16,128]{2,1,0:T(8,128)S(1)}, u32[]{:S(2)}) copy-start(f32[13,16,128]{2,1,0:T(8,128)S(1)} %collective-permute-done.9.refs_5_) | copy-start | bytes 319492
  37.6 0.7 %copy-start.5 = (f32[13,16,128]{2,1,0:T(8,128)}, f32[13,16,128]{2,1,0:T(8,128)S(1)}, u32[]{:S(2)}) copy-start(f32[13,16,128]{2,1,0:T(8,128)S(1)} %collective-permute-done.10.refs_6_) | copy-start | bytes 319492
